TPU v7x, 128 devices: a whole 4x4x4 slice. The times are simulated.
128 devices in a mesh: dp: 16 (over x, y_lo, core), tensor: 8 (over y_hi, z).
Axes of the slice: x: 4, y: 4 (y_hi: 2, y_lo: 2; y = y_hi * 2 + y_lo), z: 4, core: 2. Of those that a mesh axis runs over, the one named last changes fastest.
Arguments:
- block_input: float32 [16384, 2048], P(('dp', 'tensor')), may hold values from -6 to 6
- segments: int32 [16384], P('dp'), may hold values from 0 to 63, as said below
- positions: int32 [16384], P('dp'), may hold values from 0 to 1086, as said below
- attn_gain: float32 [2048], replicated, may hold values from 0.5 to 1.5
- w_query: bfloat16 [2048, 2048], P('dp', 'tensor'), may hold values from -0.125 to 0.125
- w_key: bfloat16 [2048, 2048], P('dp', 'tensor'), may hold values from -0.125 to 0.125
- w_value: bfloat16 [2048, 2048], P('dp', 'tensor'), may hold values from -0.125 to 0.125
- w_output: bfloat16 [2048, 2048], P('tensor', 'dp'), may hold values from -2 to 2
- mlp_gain: float32 [2048], replicated, may hold values from 0.5 to 1.5
- w_gate: bfloat16 [2048, 5504], P('dp', 'tensor'), may hold values from -0.125 to 0.125
- w_up: bfloat16 [2048, 5504], P('dp', 'tensor'), may hold values from -0.125 to 0.125
- w_down: bfloat16 [5504, 2048], P('tensor', 'dp'), may hold values from -0.078125 to 0.078125
- cotangent: float32 [16384, 2048], P(('dp', 'tensor')), may hold values from -24 to 24
Outputs:
- out_block: float32 [16384, 2048], P(('dp', 'tensor'))
- grad_input: float32 [16384, 2048], P(('dp', 'tensor'))
- grad_attn_gain: float32 [2048], replicated
- grad_query: float32 [2048, 2048], P('dp', 'tensor')
- grad_key: float32 [2048, 2048], P('dp', 'tensor')
- grad_value: float32 [2048, 2048], P('dp', 'tensor')
- grad_output: float32 [2048, 2048], P('tensor', 'dp')
- grad_mlp_gain: float32 [2048], replicated
- grad_gate: float32 [2048, 5504], P('dp', 'tensor')
- grad_up: float32 [2048, 5504], P('dp', 'tensor')
- grad_down: float32 [5504, 2048], P('tensor', 'dp')
Inputs may be any that keep to these rules, and one draw needn't show every extreme that they name: `segments`: each sequence of 1024 tokens holds four documents in order, numbered 4 * (the sequence's index) + 0, 1, 2, 3; the first has at most 64 tokens and the last two together at most 65. `positions`: positions rise by one from token to token within a document; documents 1 to 3 of a sequence start at 0, the first may continue one begun earlier and start higher.
All inputs are finite; a program needn't handle non-finite values.
Results may differ from a plain program's by a relative error of at most 0.022.
Values may be sent and summed in bfloat16 or wider, within the bound.
No kernel may reach another device: no remote copies, remote signals or barrier semaphores. Data moves between devices by JAX's collectives and lax.ppermute only.
A program may use at most 128 MiB of HBM per device.

v0:
```python
import jax
import jax.numpy as jnp
from jax import lax
from jax.sharding import PartitionSpec as P

HEAD_DIM = 128
LEN = 1024


epsilon = 1e-05
base_freq = 10000.0
contract_last = (((1,), (1,)), ((), ()))
contract_first = (((0,), (0,)), ((), ()))


def norm_forward(stream, gain_vector):
    inverse_rms = lax.rsqrt(jnp.mean(stream * stream, axis=-1, keepdims=True) + epsilon)
    return (stream * inverse_rms * gain_vector, inverse_rms)


def norm_backward(stream, inverse_rms, gain_vector, gradient):
    scaled = gradient * gain_vector
    mean_term = jnp.mean(scaled * stream, axis=-1, keepdims=True)
    cubed = inverse_rms * inverse_rms * inverse_rms
    return (
        inverse_rms * scaled - stream * cubed * mean_term,
        jnp.sum(gradient * stream * inverse_rms, axis=0),
    )


def rotary_tables(token_positions):
    half_dim = HEAD_DIM // 2
    frequency = base_freq ** (-(2.0 * jnp.arange(half_dim, dtype=jnp.float32)) / HEAD_DIM)
    angles = token_positions.astype(jnp.float32)[:, None] * frequency[None, :]
    return (jnp.cos(angles)[:, None, :], jnp.sin(angles)[:, None, :])


def rotate(vectors, cosine, sine_table):
    first_half, second_half = jnp.split(vectors, 2, axis=-1)
    return jnp.concatenate(
        [
            first_half * cosine - second_half * sine_table,
            second_half * cosine + first_half * sine_table,
        ],
        axis=-1,
    )


def rotate_back(gradient, cosine, sine_table):
    first_half, second_half = jnp.split(gradient, 2, axis=-1)
    return jnp.concatenate(
        [
            first_half * cosine + second_half * sine_table,
            second_half * cosine - first_half * sine_table,
        ],
        axis=-1,
    )


def block_scores(query_block, key_rows, seg_seq, first_row):
    block_rows = query_block.shape[0]
    logits = jnp.einsum(
        "qhd,khd->hqk", query_block, key_rows, preferred_element_type=jnp.float32
    ) * HEAD_DIM ** (-0.5)
    query_index = first_row + jnp.arange(block_rows, dtype=jnp.int32)
    key_index = jnp.arange(seg_seq.shape[0], dtype=jnp.int32)
    query_seg = lax.dynamic_slice_in_dim(seg_seq, first_row, block_rows, 0)
    allowed = (query_seg[:, None] == seg_seq[None, :]) & (
        key_index[None, :] <= query_index[:, None]
    )
    return jnp.where(allowed[None], logits, -1e30)


def attend_forward(inputs):
    queries, key_rows, value_rows, seg_seq = inputs
    block_rows = min(512, LEN)

    def one_block(first_row):
        query_block = lax.dynamic_slice_in_dim(queries, first_row, block_rows, 0)
        logits = block_scores(query_block, key_rows, seg_seq, first_row)
        row_max = jnp.max(logits, axis=-1, keepdims=True)
        exponent = jnp.exp(logits - row_max)
        row_total = jnp.sum(exponent, axis=-1, keepdims=True)
        softmax_low = (exponent / row_total).astype(jnp.bfloat16)
        result = jnp.einsum(
            "hqk,khd->qhd", softmax_low, value_rows, preferred_element_type=jnp.float32
        )
        return (result.astype(jnp.bfloat16), (row_max + jnp.log(row_total))[..., 0])

    starts = jnp.arange(LEN // block_rows, dtype=jnp.int32) * block_rows
    results, logsum = lax.map(one_block, starts)
    return (results.reshape(queries.shape), logsum)


def attend_backward(inputs):
    queries, key_rows, value_rows, seg_seq, grad_rows, logsum = inputs
    block_rows = min(512, LEN)
    scale_factor = HEAD_DIM ** (-0.5)

    def one_block(running, block_inputs):
        first_row, block_logsum = block_inputs
        key_acc, value_acc = running
        query_block = lax.dynamic_slice_in_dim(queries, first_row, block_rows, 0)
        grad_block = lax.dynamic_slice_in_dim(grad_rows, first_row, block_rows, 0)
        logits = block_scores(query_block, key_rows, seg_seq, first_row)
        softmax_rows = jnp.exp(logits - block_logsum[..., None])
        grad_probs = jnp.einsum(
            "qhd,khd->hqk", grad_block, value_rows, preferred_element_type=jnp.float32
        )
        row_inner = jnp.sum(softmax_rows * grad_probs, axis=-1, keepdims=True)
        score_grad = (softmax_rows * (grad_probs - row_inner)).astype(jnp.bfloat16)
        query_part = (
            jnp.einsum("hqk,khd->qhd", score_grad, key_rows, preferred_element_type=jnp.float32)
            * scale_factor
        )
        key_acc = (
            key_acc
            + jnp.einsum(
                "hqk,qhd->khd", score_grad, query_block, preferred_element_type=jnp.float32
            )
            * scale_factor
        )
        value_acc = value_acc + jnp.einsum(
            "hqk,qhd->khd",
            softmax_rows.astype(jnp.bfloat16),
            grad_block,
            preferred_element_type=jnp.float32,
        )
        return ((key_acc, value_acc), query_part)

    zero_rows = jnp.zeros(queries.shape, jnp.float32)
    starts = jnp.arange(LEN // block_rows, dtype=jnp.int32) * block_rows
    (key_grad, value_grad), query_grad = lax.scan(
        one_block, (zero_rows, zero_rows), (starts, logsum)
    )
    return (query_grad.reshape(queries.shape), key_grad, value_grad)


def body(
    block_input,
    segments,
    positions,
    attn_gain,
    w_query,
    w_key,
    w_value,
    w_output,
    mlp_gain,
    w_gate,
    w_up,
    w_down,
    cotangent,
):
    width_local = w_query.shape[1]
    heads_local = width_local // HEAD_DIM
    seqs_here = segments.shape[0] // LEN
    total_rows = segments.shape[0]
    shape_heads = (total_rows, heads_local, HEAD_DIM)
    shape_seqs = (seqs_here, LEN, heads_local, HEAD_DIM)
    seg_rows = segments.reshape(seqs_here, LEN)
    cosine, sine_table = rotary_tables(positions)
    normed_first, inverse_first = norm_forward(block_input, attn_gain)
    act_first = normed_first.astype(jnp.bfloat16)
    full_query, full_key, full_value, full_output = (
        lax.all_gather(w_query, "dp", axis=0, tiled=True),
        lax.all_gather(w_key, "dp", axis=0, tiled=True),
        lax.all_gather(w_value, "dp", axis=0, tiled=True),
        lax.all_gather(w_output, "dp", axis=1, tiled=True),
    )
    joined = jnp.concatenate([full_query, full_key, full_value], axis=1)
    act_first_all = lax.all_gather(act_first, "tensor", axis=0, tiled=True)
    projected = jnp.dot(act_first_all, joined, preferred_element_type=jnp.float32)
    queries = rotate(projected[:, :width_local].reshape(shape_heads), cosine, sine_table).astype(
        jnp.bfloat16
    )
    key_rows = rotate(
        projected[:, width_local : 2 * width_local].reshape(shape_heads), cosine, sine_table
    ).astype(jnp.bfloat16)
    value_rows = projected[:, 2 * width_local :].reshape(shape_heads).astype(jnp.bfloat16)
    query_seqs = queries.reshape(shape_seqs)
    key_seqs = key_rows.reshape(shape_seqs)
    value_seqs = value_rows.reshape(shape_seqs)
    attended, logsum = lax.map(attend_forward, (query_seqs, key_seqs, value_seqs, seg_rows))
    attended = attended.reshape(total_rows, width_local)
    picked = attended
    middle = block_input + lax.psum_scatter(
        jnp.dot(picked, full_output, preferred_element_type=jnp.float32),
        "tensor",
        scatter_dimension=0,
        tiled=True,
    )
    normed_second, inverse_second = norm_forward(middle, mlp_gain)
    act_second = normed_second.astype(jnp.bfloat16)
    full_gate, full_up, full_down = (
        lax.all_gather(w_gate, "dp", axis=0, tiled=True),
        lax.all_gather(w_up, "dp", axis=0, tiled=True),
        lax.all_gather(w_down, "dp", axis=1, tiled=True),
    )
    act_second_all = lax.all_gather(act_second, "tensor", axis=0, tiled=True)
    gate_value = jnp.dot(act_second_all, full_gate, preferred_element_type=jnp.float32)
    up_value = jnp.dot(act_second_all, full_up, preferred_element_type=jnp.float32)
    sigmoid_gate = jax.nn.sigmoid(gate_value)
    hidden = (gate_value * sigmoid_gate * up_value).astype(jnp.bfloat16)
    picked = hidden
    out_block = middle + lax.psum_scatter(
        jnp.dot(picked, full_down, preferred_element_type=jnp.float32).astype(jnp.bfloat16),
        "tensor",
        scatter_dimension=0,
        tiled=True,
    ).astype(jnp.float32)
    back_query, back_key, back_value, back_output, back_gate, back_up, back_down = (
        lax.all_gather(w_query, "dp", axis=0, tiled=True),
        lax.all_gather(w_key, "dp", axis=0, tiled=True),
        lax.all_gather(w_value, "dp", axis=0, tiled=True),
        lax.all_gather(w_output, "dp", axis=1, tiled=True),
        lax.all_gather(w_gate, "dp", axis=0, tiled=True),
        lax.all_gather(w_up, "dp", axis=0, tiled=True),
        lax.all_gather(w_down, "dp", axis=1, tiled=True),
    )
    back_joined = jnp.concatenate([back_query, back_key, back_value], axis=1)
    grad_low = cotangent.astype(jnp.bfloat16)
    shard_piece = lax.all_gather(grad_low, "tensor", axis=0, tiled=True)
    piece_rows = lax.dot_general(
        shard_piece, back_down, contract_last, preferred_element_type=jnp.float32
    )
    hidden_grad = piece_rows
    down_grad = lax.dot_general(
        hidden, shard_piece, contract_first, preferred_element_type=jnp.float32
    )
    hidden_grad, down_grad = (hidden_grad, down_grad)
    gate_grad = (
        hidden_grad * up_value * sigmoid_gate * (1.0 + gate_value * (1.0 - sigmoid_gate))
    ).astype(jnp.bfloat16)
    up_grad = (hidden_grad * gate_value * sigmoid_gate).astype(jnp.bfloat16)
    grad_act_second = lax.psum_scatter(
        (
            lax.dot_general(gate_grad, back_gate, contract_last, preferred_element_type=jnp.float32)
            + lax.dot_general(up_grad, back_up, contract_last, preferred_element_type=jnp.float32)
        ).astype(jnp.bfloat16),
        "tensor",
        scatter_dimension=0,
        tiled=True,
    ).astype(jnp.float32)
    gate_weight_grad = lax.dot_general(
        act_second_all, gate_grad, contract_first, preferred_element_type=jnp.float32
    )
    up_weight_grad = lax.dot_general(
        act_second_all, up_grad, contract_first, preferred_element_type=jnp.float32
    )
    grad_gate, grad_up, grad_down = (
        lax.psum_scatter(
            gate_weight_grad.astype(jnp.bfloat16), "dp", scatter_dimension=0, tiled=True
        ).astype(jnp.float32),
        lax.psum_scatter(
            up_weight_grad.astype(jnp.bfloat16), "dp", scatter_dimension=0, tiled=True
        ).astype(jnp.float32),
        lax.psum_scatter(
            down_grad.astype(jnp.bfloat16), "dp", scatter_dimension=1, tiled=True
        ).astype(jnp.float32),
    )
    middle_back, second_gain_part = norm_backward(middle, inverse_second, mlp_gain, grad_act_second)
    grad_middle = cotangent + middle_back
    middle_low = grad_middle.astype(jnp.bfloat16)
    shard_piece = lax.all_gather(middle_low, "tensor", axis=0, tiled=True)
    piece_rows = lax.dot_general(
        shard_piece, back_output, contract_last, preferred_element_type=jnp.float32
    )
    attended_grad = piece_rows
    output_grad = lax.dot_general(
        attended, shard_piece, contract_first, preferred_element_type=jnp.float32
    )
    attended_grad, output_weight_grad = (attended_grad, output_grad)
    attended_low = attended_grad.astype(jnp.bfloat16).reshape(shape_seqs)
    query_grad, key_grad, value_grad = lax.map(
        attend_backward, (query_seqs, key_seqs, value_seqs, seg_rows, attended_low, logsum)
    )
    query_low = rotate_back(query_grad.reshape(shape_heads), cosine, sine_table).astype(
        jnp.bfloat16
    )
    key_low = rotate_back(key_grad.reshape(shape_heads), cosine, sine_table).astype(jnp.bfloat16)
    value_low = value_grad.reshape(shape_heads).astype(jnp.bfloat16)
    joined_grad = jnp.concatenate(
        [
            query_low.reshape(total_rows, width_local),
            key_low.reshape(total_rows, width_local),
            value_low.reshape(total_rows, width_local),
        ],
        axis=1,
    )
    picked = joined_grad
    grad_act_first = lax.psum_scatter(
        lax.dot_general(
            picked, back_joined, contract_last, preferred_element_type=jnp.float32
        ).astype(jnp.bfloat16),
        "tensor",
        scatter_dimension=0,
        tiled=True,
    ).astype(jnp.float32)
    joined_weight_grad = lax.dot_general(
        act_first_all, joined_grad, contract_first, preferred_element_type=jnp.float32
    )
    grad_query, grad_key, grad_value, grad_output = (
        lax.psum_scatter(
            joined_weight_grad[:, :width_local].astype(jnp.bfloat16),
            "dp",
            scatter_dimension=0,
            tiled=True,
        ).astype(jnp.float32),
        lax.psum_scatter(
            joined_weight_grad[:, width_local : 2 * width_local].astype(jnp.bfloat16),
            "dp",
            scatter_dimension=0,
            tiled=True,
        ).astype(jnp.float32),
        lax.psum_scatter(
            joined_weight_grad[:, 2 * width_local :].astype(jnp.bfloat16),
            "dp",
            scatter_dimension=0,
            tiled=True,
        ).astype(jnp.float32),
        lax.psum_scatter(
            output_weight_grad.astype(jnp.bfloat16), "dp", scatter_dimension=1, tiled=True
        ).astype(jnp.float32),
    )
    input_back, first_gain_part = norm_backward(
        block_input, inverse_first, attn_gain, grad_act_first
    )
    grad_input = grad_middle + input_back
    grad_attn_gain, grad_mlp_gain = lax.psum((first_gain_part, second_gain_part), ("dp", "tensor"))
    return (
        out_block,
        grad_input,
        grad_attn_gain,
        grad_query,
        grad_key,
        grad_value,
        grad_output,
        grad_mlp_gain,
        grad_gate,
        grad_up,
        grad_down,
    )


def solution(mesh):
    return jax.shard_map(
        body,
        mesh=mesh,
        in_specs=(
            P(("dp", "tensor"), None),
            P("dp"),
            P("dp"),
            P(),
            P("dp", "tensor"),
            P("dp", "tensor"),
            P("dp", "tensor"),
            P("tensor", "dp"),
            P(),
            P("dp", "tensor"),
            P("dp", "tensor"),
            P("tensor", "dp"),
            P(("dp", "tensor"), None),
        ),
        out_specs=(
            P(("dp", "tensor"), None),
            P(("dp", "tensor"), None),
            P(),
            P("dp", "tensor"),
            P("dp", "tensor"),
            P("dp", "tensor"),
            P("tensor", "dp"),
            P(),
            P("dp", "tensor"),
            P("dp", "tensor"),
            P("tensor", "dp"),
        ),
        check_vma=False,
    )
```

profile of v0, /device:TPU:0, one launch (start us, length us, event | category | flops | bytes accessed | tf_op | source)
XLA Modules:
  0.0 1489.6 jit_solution(14043167635216349305)
XLA Ops:
  11.9 2.2 multiply_convert_fusion.5
  14.8 1.9 multiply_cosine_fusion
  16.8 27.9 %all-gather.14.cloned.1.call-done = bf16[2048,256]{1,0:T(8,128)(2,1)} async-done(((bf16[128,256]{1,0:T(8,128)(2,1)}), bf16[2048,256]{1,0:T(8,128)(2,1)}) %all-gather.14.cloned.1.call-update) | async-done | bytes 1048592 | tf_op jit(solution)/shard_map/all_gather | solution.py:165
  44.6 2.4 constant_dynamic-update-slice_fusion.2
  47.0 31.8 %all-gather.16.cloned.1.call-done = bf16[2048,256]{1,0:T(8,128)(2,1)} async-done(((bf16[128,256]{1,0:T(8,128)(2,1)}), bf16[2048,256]{1,0:T(8,128)(2,1)}) %all-gather.16.cloned.1.call-update) | async-done | bytes 1048592 | tf_op jit(solution)/shard_map/all_gather | solution.py:166
  78.8 2.3 constant_dynamic-update-slice_fusion.1
  81.1 31.9 %all-gather.18.cloned.1.call-done = bf16[2048,256]{1,0:T(8,128)(2,1)} async-done(((bf16[128,256]{1,0:T(8,128)(2,1)}), bf16[2048,256]{1,0:T(8,128)(2,1)}) %all-gather.18.cloned.1.call-update) | async-done | bytes 1048592 | tf_op jit(solution)/shard_map/all_gather | solution.py:167
  113.0 2.3 constant_dynamic-update-slice_fusion
  115.4 72.2 %all-gather.12.cloned.1.call-done = bf16[1024,2048]{1,0:T(8,128)(2,1)} async-done(((bf16[128,2048]{1,0:T(8,128)(2,1)}), bf16[1024,2048]{1,0:T(8,128)(2,1)}) %all-gather.12.cloned.1.call-update) | async-done | bytes 4194320 | tf_op jit(solution)/shard_map/all_gather | solution.py:171
  187.5 6.2 fusion.68
  195.2 2.1 fusion.67
  199.8 2.4 copy.92
  202.1 2.4 copy.93
  205.8 2.4 subtract_convert_fusion.2
  209.3 16.4 %while.47 = (s32[]{:T(128)}, bf16[2,512,2,128]{3,2,1,0:T(2,128)(2,1)S(1)}, f32[2,2,512]{2,1,0:T(2,128)S(1)}, s32[2]{0:T(128)S(1)}, s32[1024]{0:T(1024)S(1)}, /*i...) while((s32[]{:T(128)}, ...), condition=%wide.region_4.5_spmd, body=%wide.region_1.4_spmd.sunk | while | flops 551157248 | bytes 16824504 | solution.py:91
  215.5 1.6 fusion.130
  223.7 1.7 fusion.130
  225.7 6.0 fusion.56
  233.0 111.5 %reduce-scatter.20.cloned.1.call-done = f32[128,2048]{1,0:T(8,128)} async-done(((f32[1024,2048]{1,0:T(8,128)}), f32[128,2048]{1,0:T(8,128)}) %reduce-scatter.20.cloned.1.call-update) | async-done | bytes 1048592 | tf_op jit(solution)/shard_map/reduce_scatter | solution.py:186
  350.2 33.5 %all-gather.26.cloned.1.call-done = bf16[2048,688]{0,1:T(8,128)(2,1)} async-done(((bf16[128,688]{0,1:T(8,128)(2,1)}), bf16[2048,688]{0,1:T(8,128)(2,1)}) %all-gather.26.cloned.1.call-update) | async-done | bytes 2818064 | tf_op jit(solution)/shard_map/all_gather | solution.py:196
  383.8 75.2 %all-gather.22.cloned.1.call-done = bf16[1024,2048]{1,0:T(8,128)(2,1)} async-done(((bf16[128,2048]{1,0:T(8,128)(2,1)}), bf16[1024,2048]{1,0:T(8,128)(2,1)}) %all-gather.22.cloned.1.call-update) | async-done | bytes 4194320 | tf_op jit(solution)/shard_map/all_gather | solution.py:199
  458.9 7.7 fusion.70
  466.6 31.5 %all-gather.24.cloned.1.call-done = bf16[2048,688]{0,1:T(8,128)(2,1)} async-done(((bf16[128,688]{0,1:T(8,128)(2,1)}), bf16[2048,688]{0,1:T(8,128)(2,1)}) %all-gather.24.cloned.1.call-update) | async-done | bytes 2818064 | tf_op jit(solution)/shard_map/all_gather | solution.py:195
  498.2 7.8 fusion.69
  505.9 33.9 %all-gather.28.cloned.1.call-done = bf16[688,2048]{1,0:T(8,128)(2,1)} async-done(((bf16[688,128]{1,0:T(8,128)(2,1)}), bf16[688,2048]{1,0:T(8,128)(2,1)}) %all-gather.28.cloned.1.call-update) | async-done | bytes 2818064 | tf_op jit(solution)/shard_map/all_gather | solution.py:197
  539.8 74.6 %all-gather.30.cloned.1.call-done = bf16[1024,2048]{1,0:T(8,128)(2,1)} async-done(((bf16[128,2048]{1,0:T(8,128)(2,1)}), bf16[1024,2048]{1,0:T(8,128)(2,1)}) %all-gather.30.cloned.1.call-update) | async-done | bytes 4194320 | tf_op jit(solution)/shard_map/all_gather | solution.py:222
  614.4 10.0 multiply_convert_fusion.1
  624.5 3.5 fusion.71
  628.0 5.6 add_convert_fusion
  633.7 7.7 convolution_convert_fusion
  641.5 74.7 %reduce-scatter.24.cloned.1.call-done = bf16[128,2048]{1,0:T(8,128)(2,1)} async-done(((bf16[1024,2048]{1,0:T(8,128)(2,1)}), bf16[128,2048]{1,0:T(8,128)(2,1)}) %reduce-scatter.24.cloned.1.call-update) | async-done | bytes 524304 | tf_op jit(solution)/shard_map/reduce_scatter | solution.py:235
  717.6 85.9 %reduce-scatter.22.cloned.1.call-done = bf16[128,2048]{1,0:T(8,128)(2,1)} async-done(((bf16[1024,2048]{1,0:T(8,128)(2,1)}), bf16[128,2048]{1,0:T(8,128)(2,1)}) %reduce-scatter.22.cloned.1.call-update) | async-done | bytes 524304 | tf_op jit(solution)/shard_map/reduce_scatter | solution.py:205
  803.4 3.4 fusion.62
  807.0 7.2 convolution_convert_fusion.5
  814.2 4.7 copy.84
  819.0 7.3 convolution_convert_fusion.4
  826.3 4.6 copy.80
  831.2 7.3 convolution_convert_fusion.3
  838.5 4.9 copy.82
  843.5 33.9 %all-gather.32.cloned.1.call-done = bf16[1024,2048]{1,0:T(8,128)(2,1)} async-done(((bf16[128,2048]{1,0:T(8,128)(2,1)}), bf16[1024,2048]{1,0:T(8,128)(2,1)}) %all-gather.32.cloned.1.call-update) | async-done | bytes 4194320 | tf_op jit(solution)/shard_map/all_gather | solution.py:264
  877.4 4.4 convolution_convert_fusion.6
  881.8 2.3 copy.78
  884.2 3.9 convolution_convert_fusion.7
  888.1 24.1 %while.48 = (s32[]{:T(128)}, f32[1024,2,128]{0,2,1:T(8,128)S(1)}, f32[1024,2,128]{0,2,1:T(8,128)}, f32[2,512,2,128]{3,1,0,2:T(8,128)}, s32[2]{0:T(128)S(1)}, /*i...) while((s32[]{:T(128)}, f32[1024,2,128]{0,2,1:T(8,128)S(1)}, ...), condition=%wide.region_12.13_spmd.clone, body=%wide.region_10.12_spmd.clone.sunk | while | flops 1360920064 | bytes 49326364 | solution.py:133
  892.8 1.6 fusion.143
  894.4 2.0 multiply_reduce_fusion.4
  904.7 1.6 fusion.143
  906.3 2.0 multiply_reduce_fusion.4
  910.4 1.5 fusion.144
  912.2 2.2 convert_element_type.135
  914.7 2.3 add_convert_fusion.2
  918.1 5.8 convolution_convert_fusion.2
  923.9 1.7 fusion.64
  927.0 7.0 convolution_convert_fusion.1
  934.1 9.1 reduce-scatter.40.cloned.1.call-done
  945.1 64.7 %reduce-scatter.36.cloned.1.call-done = bf16[128,688]{1,0:T(8,128)(2,1)} async-done(((bf16[2048,688]{1,0:T(8,128)(2,1)}), bf16[128,688]{1,0:T(8,128)(2,1)}) %reduce-scatter.36.cloned.1.call-update) | async-done | bytes 176144
  1011.6 64.7 %reduce-scatter.38.cloned.1.call-done = bf16[128,688]{1,0:T(8,128)(2,1)} async-done(((bf16[2048,688]{1,0:T(8,128)(2,1)}), bf16[128,688]{1,0:T(8,128)(2,1)}) %reduce-scatter.38.cloned.1.call-update) | async-done | bytes 176144
  1078.2 60.5 %reduce-scatter.34.cloned.1.call-done = bf16[128,256]{1,0:T(8,128)(2,1)} async-done(((bf16[2048,256]{1,0:T(8,128)(2,1)}), bf16[128,256]{1,0:T(8,128)(2,1)}) %reduce-scatter.34.cloned.1.call-update) | async-done | bytes 65552
  1140.3 60.8 %reduce-scatter.28.cloned.1.call-done = bf16[128,256]{1,0:T(8,128)(2,1)} async-done(((bf16[2048,256]{1,0:T(8,128)(2,1)}), bf16[128,256]{1,0:T(8,128)(2,1)}) %reduce-scatter.28.cloned.1.call-update) | async-done | bytes 65552 | tf_op jit(solution)/shard_map/reduce_scatter | solution.py:303
  1202.6 61.0 %reduce-scatter.30.cloned.1.call-done = bf16[128,256]{1,0:T(8,128)(2,1)} async-done(((bf16[2048,256]{1,0:T(8,128)(2,1)}), bf16[128,256]{1,0:T(8,128)(2,1)}) %reduce-scatter.30.cloned.1.call-update) | async-done | bytes 65552 | tf_op jit(solution)/shard_map/reduce_scatter | solution.py:309
  1265.1 60.9 %reduce-scatter.32.cloned.1.call-done = bf16[128,256]{1,0:T(8,128)(2,1)} async-done(((bf16[2048,256]{1,0:T(8,128)(2,1)}), bf16[128,256]{1,0:T(8,128)(2,1)}) %reduce-scatter.32.cloned.1.call-update) | async-done | bytes 65552 | tf_op jit(solution)/shard_map/reduce_scatter | solution.py:315
  1327.5 86.4 %reduce-scatter.26.cloned.1.call-done = bf16[128,2048]{1,0:T(8,128)(2,1)} async-done(((bf16[1024,2048]{1,0:T(8,128)(2,1)}), bf16[128,2048]{1,0:T(8,128)(2,1)}) %reduce-scatter.26.cloned.1.call-update) | async-done | bytes 524304 | tf_op jit(solution)/shard_map/reduce_scatter | solution.py:291
  1415.3 64.7 %all-reduce = (f32[2048]{0:T(1024)}, f32[2048]{0:T(1024)}) all-reduce(f32[2048]{0:T(1024)S(1)} %get-tuple-element.283, f32[2048]{0:T(1024)S(1)} %get-tuple-element.281), channel_id=1, replica_groups=mesh['dp'=16,'tensor'=8] {'dp','tensor'}, use_global_device_ids=true, to_apply=%region_16.17 | all-reduce | flops 4096 | bytes 32768 | tf_op jit(solution)/shard_map/psum | solution.py:329
  1480.0 2.3 fusion.46
  (177 shorter events, 56.4 us)
Async XLA Ops:
  7.2 7.7 copy-start.21
  7.2 37.4 %all-gather.14.cloned.1.call-start = ((), (), s32[]{:S(2)}) async-start(), calls=%async_computation.12 | async-start | bytes 1114112 | tf_op jit(solution)/shard_map/all_gather | solution.py:165
  7.9 70.9 %all-gather.16.cloned.1.call-start = ((), (), s32[]{:S(2)}) async-start(), calls=%async_computation.13 | async-start | bytes 1114112 | tf_op jit(solution)/shard_map/all_gather | solution.py:166
  8.7 104.4 %all-gather.18.cloned.1.call-start = ((), (), s32[]{:S(2)}) async-start(), calls=%async_computation.14 | async-start | bytes 1114112 | tf_op jit(solution)/shard_map/all_gather | solution.py:167
  9.4 178.1 %all-gather.12.cloned.1.call-start = ((), (), s32[]{:S(2)}) async-start(), calls=%async_computation.11 | async-start | bytes 4718592 | tf_op jit(solution)/shard_map/all_gather | solution.py:171
  11.4 0.5 copy-start.19
  14.1 211.6 %all-gather.20.cloned.1.call-start = ((), (), s32[]{:S(2)}) async-start(), calls=%async_computation.15 | async-start | bytes 1114112 | tf_op jit(solution)/shard_map/all_gather | solution.py:168
  14.7 329.8 %reduce-scatter.20.cloned.1.call-start = ((), (), s32[]{:S(2)}) async-start(), calls=%async_computation.16 | async-start | bytes 9437184 | tf_op jit(solution)/shard_map/reduce_scatter | solution.py:186
  16.7 189.1 %copy-start.4 = (f32[1024,64]{1,0:T(8,128)}, f32[1024,64]{1,0:T(8,128)S(1)}, u32[]{:S(2)}) copy-start(f32[1024,64]{1,0:T(8,128)S(1)} %get-tuple-element.358) | copy-start | bytes 786436
  16.7 189.1 %copy-start.6 = (f32[1024,64]{1,0:T(8,128)}, f32[1024,64]{1,0:T(8,128)S(1)}, u32[]{:S(2)}) copy-start(f32[1024,64]{1,0:T(8,128)S(1)} %get-tuple-element.359) | copy-start | bytes 786436
  208.3 0.7 copy-start.12
  208.3 1.0 copy-start.13
  225.7 6.0 copy-start.14
  231.7 112.8 %copy-start = (f32[128,2048]{1,0:T(8,128)S(1)}, f32[128,2048]{1,0:T(8,128)}, u32[]{:S(2)}) copy-start(f32[128,2048]{1,0:T(8,128)} %param.17) | copy-start | bytes 3145732
  231.7 115.2 %copy-start.17 = (f32[2048]{0:T(1024)S(1)}, f32[2048]{0:T(1024)}, u32[]{:S(2)}) copy-start(f32[2048]{0:T(1024)} %param.25) | copy-start | bytes 24580
  231.7 152.1 %all-gather.26.cloned.1.call-start = ((), (), s32[]{:S(2)}) async-start(), calls=%async_computation.19 | async-start | bytes 2994176 | tf_op jit(solution)/shard_map/all_gather | solution.py:196
  232.5 226.5 %all-gather.22.cloned.1.call-start = ((), (), s32[]{:S(2)}) async-start(), calls=%async_computation.17 | async-start | bytes 4718592 | tf_op jit(solution)/shard_map/all_gather | solution.py:199
  345.9 1.0 copy-start.2
  345.9 3.3 copy-start.9
  347.9 150.3 %all-gather.24.cloned.1.call-start = ((), (), s32[]{:S(2)}) async-start(), calls=%async_computation.18 | async-start | bytes 2994176 | tf_op jit(solution)/shard_map/all_gather | solution.py:195
  348.6 191.2 %all-gather.28.cloned.1.call-start = ((), (), s32[]{:S(2)}) async-start(), calls=%async_computation.20 | async-start | bytes 2994176 | tf_op jit(solution)/shard_map/all_gather | solution.py:197
  349.2 265.2 %all-gather.30.cloned.1.call-start = ((), (), s32[]{:S(2)}) async-start(), calls=%async_computation.22 | async-start | bytes 4718592 | tf_op jit(solution)/shard_map/all_gather | solution.py:222
  350.2 366.0 %reduce-scatter.24.cloned.1.call-start = ((), (), s32[]{:S(2)}) async-start(), calls=%async_computation.23 | async-start | bytes 4718592 | tf_op jit(solution)/shard_map/reduce_scatter | solution.py:235
  614.4 10.0 copy-start.24
  624.5 3.6 copy-start.25
  624.5 3.6 copy-start.26
  624.5 3.6 copy-start.23
  633.7 169.8 %reduce-scatter.22.cloned.1.call-start = ((), (), s32[]{:S(2)}) async-start(), calls=%async_computation.21 | async-start | bytes 4718592 | tf_op jit(solution)/shard_map/reduce_scatter | solution.py:205
  641.4 74.8 %copy-start.3 = (f32[128,2048]{1,0:T(8,128)S(1)}, f32[128,2048]{1,0:T(8,128)}, u32[]{:S(2)}) copy-start(f32[128,2048]{1,0:T(8,128)} %copy-done.2) | copy-start | bytes 3145732
  641.4 236.0 %all-gather.32.cloned.1.call-start = ((), (), s32[]{:S(2)}) async-start(), calls=%async_computation.24 | async-start | bytes 4718592 | tf_op jit(solution)/shard_map/all_gather | solution.py:264
  806.9 136.3 %reduce-scatter.40.cloned.1.call-start = ((), (), s32[]{:S(2)}) async-start(), calls=%async_computation.32 | async-start | bytes 3342336
  819.0 190.8 %reduce-scatter.36.cloned.1.call-start = ((), (), s32[]{:S(2)}) async-start(), calls=%async_computation.30 | async-start | bytes 3342336
  831.0 245.4 %reduce-scatter.38.cloned.1.call-start = ((), (), s32[]{:S(2)}) async-start(), calls=%async_computation.31 | async-start | bytes 3342336
  838.5 38.9 %copy-start.15 = (bf16[2,512,2,128]{3,2,1,0:T(2,128)(2,1)S(1)}, bf16[2,512,2,128]{3,2,1,0:T(2,128)(2,1)}, u32[]{:S(2)}) copy-start(bf16[2,512,2,128]{3,2,1,0:T(2,128)(2,1)} %copy-done.14) | copy-start | bytes 1572868
  843.4 295.3 %reduce-scatter.34.cloned.1.call-start = ((), (), s32[]{:S(2)}) async-start(), calls=%async_computation.29 | async-start | bytes 1114112
  884.1 317.0 %reduce-scatter.28.cloned.1.call-start = ((), (), s32[]{:S(2)}) async-start(), calls=%async_computation.26 | async-start | bytes 1114112 | tf_op jit(solution)/shard_map/reduce_scatter | solution.py:303
  890.6 2.1 copy-start.10
  894.4 2.0 copy-start.11
  902.5 2.1 copy-start.10
  906.3 2.0 copy-start.11
  912.1 2.5 copy-start.5
  912.2 2.5 copy-start.7
  917.0 1.1 copy-start.16
  925.6 338.0 %reduce-scatter.30.cloned.1.call-start = ((), (), s32[]{:S(2)}) async-start(), calls=%async_computation.27 | async-start | bytes 1114112 | tf_op jit(solution)/shard_map/reduce_scatter | solution.py:309
  926.2 399.7 %reduce-scatter.32.cloned.1.call-start = ((), (), s32[]{:S(2)}) async-start(), calls=%async_computation.28 | async-start | bytes 1114112 | tf_op jit(solution)/shard_map/reduce_scatter | solution.py:315
  927.0 486.9 %reduce-scatter.26.cloned.1.call-start = ((), (), s32[]{:S(2)}) async-start(), calls=%async_computation.25 | async-start | bytes 4718592 | tf_op jit(solution)/shard_map/reduce_scatter | solution.py:291
  934.0 479.8 %copy-start.1 = (f32[128,2048]{1,0:T(8,128)S(1)}, f32[128,2048]{1,0:T(8,128)}, u32[]{:S(2)}) copy-start(f32[128,2048]{1,0:T(8,128)} %param.17) | copy-start | bytes 3145732
  934.0 479.8 %copy-start.18 = (f32[2048]{0:T(1024)S(1)}, f32[2048]{0:T(1024)}, u32[]{:S(2)}) copy-start(f32[2048]{0:T(1024)} %param.20) | copy-start | bytes 24580
  934.0 479.8 %copy-start.20 = (f32[128]{0:T(128)S(1)}, f32[128]{0:T(128)}, u32[]{:S(2)}) copy-start(f32[128]{0:T(128)} %copy-done.19) | copy-start | bytes 1540
  934.1 545.9 %copy-start.8 = (f32[128,2048]{1,0:T(8,128)S(1)}, f32[128,2048]{1,0:T(8,128)}, u32[]{:S(2)}) copy-start(f32[128,2048]{1,0:T(8,128)} %get-tuple-element.326) | copy-start | bytes 3145732
  934.1 545.9 %copy-start.22 = (f32[128]{0:T(128)S(1)}, f32[128]{0:T(128)}, u32[]{:S(2)}) copy-start(f32[128]{0:T(128)} %get-tuple-element.360) | copy-start | bytes 1540
Sparse Core Ops, SparseCore 0:
  9.7 34.8 all-gather.13
  46.3 32.4 all-gather.15
  80.5 32.4 all-gather.17
  115.8 71.6 all-gather.11
  189.0 31.6 all-gather.19
  231.8 112.6 reduce-scatter.19
  346.2 37.5 all-gather.25
  387.0 71.9 all-gather.21
  460.6 37.4 all-gather.23
  499.7 40.0 all-gather.27
  542.5 71.9 all-gather.29
  633.8 82.3 reduce-scatter.23
  720.0 83.4 reduce-scatter.21
  807.0 70.3 all-gather.31
  879.8 63.3 reduce-scatter.39
  945.6 64.1 reduce-scatter.35
  1012.2 64.1 reduce-scatter.37
  1078.7 59.9 reduce-scatter.33
  1141.1 59.9 reduce-scatter.27
  1203.5 60.0 reduce-scatter.29
  1266.0 59.9 reduce-scatter.31
  1330.3 83.5 reduce-scatter.25
where the time goes:
time: 1500 us; the launch traced here: 1490 us
  waiting for transfers between devices  1190 us (79%)
  matrix products  116 us (8%)
  blocking collectives  64.7 us (4%)
  local copies, waits for them, and re-layouts  47.6 us (3%)
  other arithmetic  43.7 us (3%)
  between operations  15.2 us (1%)
    unnamed x26, waiting for transfers between devices  205 us
    reduce_scatter x1, waiting for transfers between devices, body(): lax.psum_scatter(jnp.dot(picked, full_output, preferred_element_type=jnp....  112 us
    reduce_scatter x1, waiting for transfers between devices, body(): lax.psum_scatter(lax.dot_general(picked, back_joined, contract_last, pref...  86.4 us
    reduce_scatter x1, waiting for transfers between devices, body(): lax.psum_scatter(jnp.dot(picked, full_down, preferred_element_type=jnp.fl...  85.9 us
    all_gather x1, waiting for transfers between devices, body(): act_second_all = lax.all_gather(act_second, 'tensor', axis=0, tiled=True)  75.2 us
    reduce_scatter x1, waiting for transfers between devices, body(): lax.psum_scatter((lax.dot_general(gate_grad, back_gate, contract_last, pr...  74.7 us
    all_gather x1, waiting for transfers between devices, body(): shard_piece = lax.all_gather(grad_low, 'tensor', axis=0, tiled=True)  74.6 us
    all_gather x1, waiting for transfers between devices, body(): act_first_all = lax.all_gather(act_first, 'tensor', axis=0, tiled=True)  72.2 us
  transfers between devices with their start and end apart: 22, of which 21 were waited for; matrix products, arithmetic and copies ran while one was open for 12% of the time, Pallas kernels for 0%

commit v1 on v0

v1 whole, which is shorter than its diff:
```python
import jax
import jax.numpy as jnp
import numpy as np
from jax import lax
from jax.sharding import Mesh, PartitionSpec as P

HEAD_DIM = 128
LEN = 1024
BLOCK = 128
epsilon = 1e-05
base_freq = 10000.0
AXES = ("x", "ylo", "core", "yhi", "z")
SIZES = {"x": 4, "ylo": 2, "core": 2, "yhi": 2, "z": 4}
bf16 = jnp.bfloat16
f32 = jnp.float32
contract_last = (((1,), (1,)), ((), ()))
contract_first = (((0,), (0,)), ((), ()))


def swap_bits(value, axes, masks):
    sizes = [SIZES[a] for a in axes]
    pairs = []
    for index in np.ndindex(*sizes):
        target = tuple(i ^ m for i, m in zip(index, masks))
        pairs.append(
            (int(np.ravel_multi_index(index, sizes)), int(np.ravel_multi_index(target, sizes)))
        )
    return lax.ppermute(value, axes if len(axes) > 1 else axes[0], pairs)


def over_x(value, k):
    return swap_bits(value, ("x",), (k,))


def over_y(value, low, high):
    return swap_bits(value, ("ylo", "yhi"), (low, high))


def over_z(value, k):
    return swap_bits(value, ("z",), (k,))


def over_core(value):
    return swap_bits(value, ("core",), (1,))


def exchange(value):
    return lax.ppermute(value, ("core", "yhi"), [(0, 0), (1, 2), (2, 1), (3, 3)])


Y_STEPS = ((0, 1), (1, 0), (1, 1))


def gather_x_first(piece):
    row = jnp.concatenate([piece] + [over_x(piece, k) for k in (1, 2, 3)], axis=1)
    got = {(0, 0): row}
    for low, high in Y_STEPS:
        got[(low, high)] = over_y(row, low, high)
    return [
        jnp.concatenate(
            [got[(low, high)][:, 128 * i : 128 * i + 128] for i in range(4) for low in range(2)],
            axis=1,
        )
        for high in range(2)
    ]


def gather_y_first(piece):
    rows = piece.shape[0]
    got = {(0, 0): piece}
    for low, high in Y_STEPS:
        got[(low, high)] = over_y(piece, low, high)
    block = jnp.concatenate(
        [jnp.concatenate([got[(0, high)], got[(1, high)]], axis=1) for high in range(2)], axis=0
    )
    full = jnp.concatenate([block] + [over_x(block, k) for k in (1, 2, 3)], axis=1)
    return [full[:rows], full[rows:]]


def scatter_x_first(total):
    def part(low, high):
        return jnp.concatenate(
            [total[high][:, 256 * i + 128 * low : 256 * i + 128 * low + 128] for i in range(4)],
            axis=1,
        )

    acc = part(0, 0).astype(f32)
    for low, high in Y_STEPS:
        acc = acc + over_y(part(low, high).astype(bf16), low, high).astype(f32)
    out = acc[:, :128]
    for k in (1, 2, 3):
        out = out + over_x(acc[:, 128 * k : 128 * k + 128].astype(bf16), k).astype(f32)
    return out


def scatter_y_first(total):
    rows = total[0].shape[0]
    both = jnp.concatenate(total, axis=0)
    acc = both[:, :256].astype(f32)
    for k in (1, 2, 3):
        acc = acc + over_x(both[:, 256 * k : 256 * k + 256].astype(bf16), k).astype(f32)
    out = acc[:rows, :128]
    for low, high in Y_STEPS:
        out = out + over_y(
            acc[rows * high : rows * high + rows, 128 * low : 128 * low + 128].astype(bf16),
            low,
            high,
        ).astype(f32)
    return out


def gather_tokens(value):
    return jnp.concatenate([value] + [over_z(value, k) for k in (1, 2, 3)], axis=0)


def scatter_tokens(value):
    out = value[:BLOCK].astype(f32)
    for k in (1, 2, 3):
        out = out + over_z(value[BLOCK * k : BLOCK * k + BLOCK].astype(bf16), k).astype(f32)
    return out


def norm_forward(stream, gain):
    inverse = lax.rsqrt(jnp.mean(stream * stream, axis=-1, keepdims=True) + epsilon)
    return (stream * inverse * gain).astype(bf16), inverse


def norm_backward(stream, inverse, gain, gradient):
    scaled = gradient * gain
    mean_term = jnp.mean(scaled * stream, axis=-1, keepdims=True)
    back = inverse * scaled - stream * (inverse * inverse * inverse) * mean_term
    return back, jnp.sum(gradient * stream * inverse, axis=0)


def rotate(vectors, cosine, sine):
    first, second = jnp.split(vectors, 2, axis=-1)
    return jnp.concatenate([first * cosine - second * sine, second * cosine + first * sine], -1)


def dot_nt(left, halves):
    own, other = halves
    half = left.shape[1] // 2
    return lax.dot_general(
        left[:, :half], own, contract_last, preferred_element_type=f32
    ) + lax.dot_general(left[:, half:], other, contract_last, preferred_element_type=f32)


def dot_nn(left, halves):
    return jnp.concatenate(
        [jnp.dot(left, w, preferred_element_type=f32).astype(bf16) for w in halves], axis=1
    )


def grad_halves(left, right):
    half = right.shape[1] // 2
    away = lax.dot_general(
        left, right[:, half:], contract_first, preferred_element_type=f32
    ).astype(bf16)
    here = lax.dot_general(left, right[:, :half], contract_first, preferred_element_type=f32)
    return here + over_core(away).astype(f32)


def body(
    block_input,
    segments,
    positions,
    attn_gain,
    w_query,
    w_key,
    w_value,
    w_output,
    mlp_gain,
    w_gate,
    w_up,
    w_down,
    cotangent,
):
    at_x, at_ylo, at_core, at_yhi, at_z = (lax.axis_index(a) for a in AXES)
    width = w_query.shape[1]
    hidden_local = w_gate.shape[1]
    first_core = at_core == 0

    def reorder(value):
        parts = []
        for k in range(2):
            for i in range(4):
                for j in range(2):
                    index = (at_x ^ i) * 4 + (at_ylo ^ j) * 2 + (at_core ^ k)
                    parts.append(lax.dynamic_slice_in_dim(value, index * 128, 128, axis=-1))
        return jnp.concatenate(parts, axis=-1)

    def restore(value):
        parts = []
        for x in range(4):
            for y in range(2):
                for c in range(2):
                    index = (at_core ^ c) * 8 + (at_x ^ x) * 2 + (at_ylo ^ y)
                    parts.append(lax.dynamic_slice_in_dim(value, index * 128, 128, axis=-1))
        return jnp.concatenate(parts, axis=-1)

    piece_qk = jnp.concatenate([w_query.T, w_key.T], axis=0)
    piece_vo = jnp.concatenate([w_value.T, w_output], axis=0)
    cut = 352
    piece_gd = jnp.concatenate([w_gate.T, w_down[:cut]], axis=0)
    piece_ud = jnp.concatenate([w_up.T, w_down[cut:]], axis=0)

    stream = reorder(exchange(block_input))
    grad_low = reorder(exchange(cotangent.astype(bf16)))
    tables = jnp.stack([segments, positions])
    tables = jnp.where(at_core == at_yhi, tables, over_core(tables))
    gain1 = reorder(attn_gain)
    gain2 = reorder(mlp_gain)

    qk = gather_x_first(piece_qk)
    vo = gather_y_first(piece_vo)

    def both(parts):
        own = jnp.concatenate(parts, axis=0)
        return own, over_core(own)

    weight_q = both([p[:width] for p in qk])
    weight_k = both([p[width:] for p in qk])
    weight_v = both([p[:width] for p in vo])
    weight_o = both([p[width:] for p in vo])

    act1, inverse1 = norm_forward(stream, gain1)
    act1_all = gather_tokens(act1)

    order = [(at_core ^ h) * 4 + (at_z ^ k) for h in range(2) for k in range(4)]
    tables = jnp.concatenate(
        [lax.dynamic_slice_in_dim(tables, o * BLOCK, BLOCK, axis=1) for o in order], axis=1
    )
    place = jnp.concatenate([o * BLOCK + jnp.arange(BLOCK, dtype=jnp.int32) for o in order])
    seg_rows, pos_rows = tables[0], tables[1]
    frequency = base_freq ** (-(2.0 * jnp.arange(HEAD_DIM // 2, dtype=f32)) / HEAD_DIM)
    angles = pos_rows[:512].astype(f32)[:, None] * frequency[None, :]
    cosine, sine = jnp.cos(angles)[:, None, :], jnp.sin(angles)[:, None, :]

    def heads(value):
        return value.reshape(512, -1, HEAD_DIM)

    q = rotate(heads(dot_nt(act1_all, weight_q)), cosine, sine).astype(bf16)
    k = rotate(heads(dot_nt(act1_all, weight_k)), cosine, sine).astype(bf16)
    v = heads(dot_nt(act1_all, weight_v)).astype(bf16)
    qkv = jnp.stack([q, k, v]).reshape(3, 512, 2, 2, HEAD_DIM)
    keep = jnp.where(first_core, qkv[:, :, 0], qkv[:, :, 1])
    away = jnp.where(first_core, qkv[:, :, 1], qkv[:, :, 0])
    qkv = jnp.concatenate([keep, over_core(away)], axis=1)
    queries, keys, values = qkv[0], qkv[1], qkv[2]

    allowed = (seg_rows[:, None] == seg_rows[None, :]) & (place[None, :] <= place[:, None])
    scale = HEAD_DIM**-0.5
    logits = jnp.einsum("qhd,khd->hqk", queries, keys, preferred_element_type=f32) * scale
    logits = jnp.where(allowed[None], logits, -1e30)
    row_max = jnp.max(logits, axis=-1, keepdims=True)
    exponent = jnp.exp(logits - row_max)
    probs = exponent / jnp.sum(exponent, axis=-1, keepdims=True)
    probs_low = probs.astype(bf16)
    attended = jnp.einsum("hqk,khd->qhd", probs_low, values, preferred_element_type=f32)
    attended = attended.astype(bf16).reshape(1024, 2 * HEAD_DIM)

    def rejoin(value):
        mine = value[..., :512, :]
        got = over_core(value[..., 512:, :])
        return jnp.concatenate(
            [jnp.where(first_core, mine, got), jnp.where(first_core, got, mine)], axis=-1
        )

    attended_rows = rejoin(attended)
    middle = stream + scatter_tokens(dot_nn(attended_rows, weight_o))
    act2, inverse2 = norm_forward(middle, gain2)
    act2_all = gather_tokens(act2)

    gd = gather_x_first(piece_gd)
    ud = gather_y_first(piece_ud)
    weight_g = both([p[:hidden_local] for p in gd])
    weight_u = both([p[:hidden_local] for p in ud])
    weight_d = both([p[hidden_local:] for pair in zip(gd, ud) for p in pair])

    grad_all = gather_tokens(grad_low)
    hidden_grad = dot_nt(grad_all, weight_d)
    gate = dot_nt(act2_all, weight_g)
    up = dot_nt(act2_all, weight_u)
    sigmoid = jax.nn.sigmoid(gate)
    silu = gate * sigmoid
    hidden = (silu * up).astype(bf16)
    gate_grad = (hidden_grad * up * sigmoid * (1.0 + gate * (1.0 - sigmoid))).astype(bf16)
    up_grad = (hidden_grad * silu).astype(bf16)

    out_block = middle + scatter_tokens(dot_nn(hidden, weight_d))
    grad_act2 = scatter_tokens(
        jnp.concatenate(
            [
                (
                    jnp.dot(gate_grad, wg, preferred_element_type=f32)
                    + jnp.dot(up_grad, wu, preferred_element_type=f32)
                ).astype(bf16)
                for wg, wu in zip(weight_g, weight_u)
            ],
            axis=1,
        )
    )
    sum_g = grad_halves(gate_grad, act2_all)
    sum_u = grad_halves(up_grad, act2_all)
    sum_d = grad_halves(hidden, grad_all)
    n = hidden_local
    grad_gd = scatter_x_first(
        [jnp.concatenate([sum_g[h * n : h * n + n], sum_d[h * n : h * n + cut]]) for h in range(2)]
    )
    grad_ud = scatter_y_first(
        [
            jnp.concatenate([sum_u[h * n : h * n + n], sum_d[h * n + cut : h * n + n]])
            for h in range(2)
        ]
    )
    grad_gate = grad_gd[:n].T
    grad_up = grad_ud[:n].T
    grad_down = jnp.concatenate([grad_gd[n:], grad_ud[n:]], axis=0)

    middle_back, gain2_part = norm_backward(middle, inverse2, gain2, grad_act2)
    grad_middle = grad_low.astype(f32) + middle_back
    middle_low = grad_middle.astype(bf16)
    middle_all = gather_tokens(middle_low)
    attended_grad = dot_nt(middle_all, weight_o).astype(bf16)
    sum_o = grad_halves(attended_rows, middle_all)
    split = attended_grad.reshape(512, 2, 256)
    keep = jnp.where(first_core, split[:, 0], split[:, 1])
    away = jnp.where(first_core, split[:, 1], split[:, 0])
    attended_grad = jnp.concatenate([keep, over_core(away)], axis=0).reshape(1024, 2, HEAD_DIM)

    grad_probs = jnp.einsum("qhd,khd->hqk", attended_grad, values, preferred_element_type=f32)
    inner = jnp.sum(probs * grad_probs, axis=-1, keepdims=True)
    score_grad = (probs * (grad_probs - inner)).astype(bf16)
    query_grad = jnp.einsum("hqk,khd->qhd", score_grad, keys, preferred_element_type=f32) * scale
    key_grad = jnp.einsum("hqk,qhd->khd", score_grad, queries, preferred_element_type=f32) * scale
    value_grad = jnp.einsum("hqk,qhd->khd", probs_low, attended_grad, preferred_element_type=f32)
    angles = pos_rows.astype(f32)[:, None] * frequency[None, :]
    cosine, sine = jnp.cos(angles)[:, None, :], jnp.sin(angles)[:, None, :]
    grads = jnp.stack(
        [
            rotate(query_grad, cosine, -sine).astype(bf16),
            rotate(key_grad, cosine, -sine).astype(bf16),
            value_grad.astype(bf16),
        ]
    ).reshape(3, 1024, 2 * HEAD_DIM)
    q_low, k_low, v_low = rejoin(grads)
    grad_act1 = scatter_tokens(
        jnp.concatenate(
            [
                sum(
                    jnp.dot(g, w, preferred_element_type=f32)
                    for g, w in ((q_low, wq), (k_low, wk), (v_low, wv))
                ).astype(bf16)
                for wq, wk, wv in zip(weight_q, weight_k, weight_v)
            ],
            axis=1,
        )
    )
    sum_q = grad_halves(q_low, act1_all)
    sum_k = grad_halves(k_low, act1_all)
    sum_v = grad_halves(v_low, act1_all)
    w = width
    grad_qk = scatter_x_first(
        [jnp.concatenate([sum_q[h * w : h * w + w], sum_k[h * w : h * w + w]]) for h in range(2)]
    )
    grad_vo = scatter_y_first(
        [jnp.concatenate([sum_v[h * w : h * w + w], sum_o[h * w : h * w + w]]) for h in range(2)]
    )
    input_back, gain1_part = norm_backward(stream, inverse1, gain1, grad_act1)
    grad_input = exchange(restore(grad_middle + input_back).astype(bf16)).astype(f32)
    out_block = exchange(restore(out_block))

    gains = restore(jnp.stack([gain1_part, gain2_part]))

    def add_four(value, step):
        one, two, three = (step(value, i) for i in range(3))
        return (value + one) + (two + three)

    gains = add_four(gains, lambda v, i: over_z(v, i + 1))
    gains = add_four(gains, lambda v, i: over_y(v, *((0, 1), (1, 0), (1, 1))[i]))
    gains = add_four(gains, lambda v, i: over_x(v, i + 1))
    gains = gains + over_core(gains)
    return (
        out_block,
        grad_input,
        gains[0],
        grad_qk[:w].T,
        grad_qk[w:].T,
        grad_vo[:w].T,
        grad_vo[w:],
        gains[1],
        grad_gate,
        grad_up,
        grad_down,
    )


def solution(mesh):
    inner = Mesh(np.asarray(mesh.devices).reshape([SIZES[a] for a in AXES]), AXES)
    dp, tensor = ("x", "ylo", "core"), ("yhi", "z")
    rows = P(dp + tensor, None)
    return jax.shard_map(
        body,
        mesh=inner,
        in_specs=(
            rows,
            P(dp),
            P(dp),
            P(),
            P(dp, tensor),
            P(dp, tensor),
            P(dp, tensor),
            P(tensor, dp),
            P(),
            P(dp, tensor),
            P(dp, tensor),
            P(tensor, dp),
            rows,
        ),
        out_specs=(
            rows,
            rows,
            P(),
            P(dp, tensor),
            P(dp, tensor),
            P(dp, tensor),
            P(tensor, dp),
            P(),
            P(dp, tensor),
            P(dp, tensor),
            P(tensor, dp),
        ),
        check_vma=False,
    )
```

time: 1500 us -> 736 us (0.49)
  waiting for transfers between devices: 1190 us -> 272 us
  starting transfers between devices: 1.56 us -> 161 us
  blocking collectives: 64.7 us -> 0 us
  other arithmetic: 43.7 us -> 93 us
  local copies, waits for them, and re-layouts: 47.6 us -> 90.6 us
    reduce_scatter x7 -> x0, waiting for transfers between devices: 541 us -> none  [the longest x1 112 us: body(): lax.psum_scatter(jnp.dot(picked, full_output, preferred_element_type=jnp....]
    all_gather x11 -> x0, waiting for transfers between devices: 446 us -> none  [the longest x1 75.2 us: body(): act_second_all = lax.all_gather(act_second, 'tensor', axis=0, tiled=True)]
    ppermute x0 -> x105, waiting for transfers between devices: none -> 272 us  [the longest x101 272 us: swap_bits(): return lax.ppermute(value, axes if len(axes) > 1 else axes[0], pairs)]
    unnamed x26 -> x0, waiting for transfers between devices: 205 us -> none
    ppermute x0 -> x105, starting transfers between devices: none -> 161 us  [the longest x101 152 us: swap_bits(): return lax.ppermute(value, axes if len(axes) > 1 else axes[0], pairs)]
    psum x1 -> x0, blocking collectives: 64.7 us -> none  [body(): lax.psum((first_gain_part, second_gain_part), ('dp', 'tensor'))]
    concatenate x3 -> x40, other arithmetic: 1.16 us -> 59 us  [the longest x7 30.1 us: both(): own = jnp.concatenate(parts, axis=0)]
    unnamed x64 -> x333, local copies, waits for them, and re-layouts: 34.9 us -> 66.7 us
  transfers between devices with their start and end apart: 22 -> 105, of which waited for: 21 -> 38; matrix products, arithmetic and copies ran while one was open for 12% -> 35% of each run, Pallas kernels for 0% -> 0%
where the time goes in v1:
time: 736 us; the launch traced here: 725 us
  waiting for transfers between devices  272 us (37%)
  starting transfers between devices  161 us (22%)
  matrix products  104 us (14%)
  other arithmetic  93 us (13%)
  local copies, waits for them, and re-layouts  90.6 us (12%)
    ppermute x101, waiting for transfers between devices, swap_bits(): return lax.ppermute(value, axes if len(axes) > 1 else axes[0], pairs)  272 us
    ppermute x101, starting transfers between devices, swap_bits(): return lax.ppermute(value, axes if len(axes) > 1 else axes[0], pairs)  152 us
    unnamed x333, local copies, waits for them, and re-layouts  66.7 us
    concatenate x7, other arithmetic, both(): own = jnp.concatenate(parts, axis=0)  30.1 us
    dot_general x7, matrix products, dot_nt(): lax.dot_general(left[:, half:], other, contract_last, preferred_element_t...  18.4 us
  transfers between devices with their start and end apart: 105, of which 38 were waited for; matrix products, arithmetic and copies ran while one was open for 35% of the time, Pallas kernels for 0%

profile of v1, /device:TPU:0, one launch (start us, length us, event | category | flops | bytes accessed | tf_op | source)
XLA Modules:
  0.0 724.7 jit_solution(14864996807188441139)
XLA Ops:
  3.1 3.1 collective-permute-start.15
  8.8 2.8 collective-permute-start.6
  47.3 3.1 collective-permute-start.38
  53.8 2.9 collective-permute-start.31
  57.5 5.0 collective-permute-done.38
  68.2 2.8 collective-permute-start.18
  71.0 6.1 collective-permute-start.8
  77.2 19.5 %collective-permute-start.9 = (bf16[512,512]{0,1:T(8,128)(2,1)S(1)}, bf16[512,512]{0,1:T(8,128)(2,1)S(1)}, u32[]{:S(2)}, u32[]{:S(2)}) collective-permute-start(bf16[512,512]{0,1:T(8,128)(2,1)S(1)} %pad_maximum_fusion.28), channel_id=1, source_target_pairs={{0,20},{4,16},{16,4},{20,0},{1,21},{5,17},{17,5},{21,1},{2,22},{6,... | collective-permute-start | bytes 1572872 | tf_op jit(solution)/shard_map/ppermute | solution.py:28
  107.3 2.6 collective-permute-done.9
  117.0 3.2 pad_maximum_fusion.8
  120.4 3.3 collective-permute-done.7
  123.7 3.6 collective-permute-start.33
  134.4 25.9 %collective-permute-done.41 = bf16[2048,256]{1,0:T(8,128)(2,1)S(1)} collective-permute-done((bf16[2048,256]{1,0:T(8,128)(2,1)S(1)}, bf16[2048,256]{1,0:T(8,128)(2,1)S(1)}, u32[]{:S(2)}, u32[]{:S(2)}) %collective-permute-start.41) | collective-permute-done | bytes 1048608 | tf_op jit(solution)/shard_map/ppermute | solution.py:28
  162.4 6.7 pad_maximum_fusion.2
  171.8 4.0 collective-permute-start.3
  177.9 6.7 collective-permute-done.32
  186.9 12.3 %collective-permute-done.3 = bf16[128,2048]{1,0:T(8,128)(2,1)S(1)} collective-permute-done((bf16[128,2048]{1,0:T(8,128)(2,1)S(1)}, bf16[128,2048]{1,0:T(8,128)(2,1)S(1)}, u32[]{:S(2)}, u32[]{:S(2)}) %collective-permute-start.3) | collective-permute-done | bytes 524320 | tf_op jit(solution)/shard_map/ppermute | solution.py:28
  199.2 3.0 collective-permute-start.51
  225.8 7.6 %fusion.199 = (f32[2,1024]{1,0:T(2,128)S(1)}, f32[2,1024,1024]{1,2,0:T(8,128)}) fusion(pred[1024,1024]{0,1:T(8,128)(4,1)} %compare_and_fusion, bf16[1024,2,128]{2,0,1:T(8,128)(2,1)S(1)} %fusion.108, bf16[3,512,2,128]{3,1,2,0:T(8,128)(2,1)S(1)} %get-tuple-element.124, bf16[3,512,2,128]{3,1,2,0:T(8,128)(2,1)S(1)} %collective-permute-done.20), kind=kOutput, calls=%fused_computation.601 | convolution fusion | flops 546309120 | bytes 11542528 | tf_op jit(solution)/shard_map/sub | solution.py:256
  233.4 4.4 fusion.50
  247.1 22.6 %fusion.21 = bf16[1376,1024]{1,0:T(8,128)(2,1)} fusion(bf16[2048,256]{1,0:T(8,128)(2,1)S(1)} %copy-done.27, bf16[2048,256]{1,0:T(8,128)(2,1)S(1)} %copy-done.29, bf16[2048,256]{1,0:T(8,128)(2,1)S(1)} %copy-done.31, bf16[1024,128]{1,0:T(8,128)(2,1)S(1)} %copy-done.42, bf16[1024,128]{1,0:T(8,128)(2,1)S(1)} %copy-done.44, bf16[1024,128]{1,0:T(8,128)(2,1)S(1)} %copy-done.46, ...), kind=kLoop, calls=%fused_computation.61 | loop fusion | flops 77496320 | bytes 8454144 | tf_op jit(solution)/shard_map/concatenate | solution.py:218
  272.6 2.7 collective-permute-start.28
  277.7 8.5 %collective-permute-done.50 = bf16[128,2048]{1,0:T(8,128)(2,1)S(1)} collective-permute-done((bf16[128,2048]{1,0:T(8,128)(2,1)}, bf16[128,2048]{1,0:T(8,128)(2,1)S(1)}, u32[]{:S(2)}, u32[]{:S(2)}) %collective-permute-start.50) | collective-permute-done | bytes 524320 | tf_op jit(solution)/shard_map/ppermute | solution.py:28
  287.1 6.7 collective-permute-done.49
  293.8 3.2 collective-permute-start.27
  300.4 10.1 %collective-permute-done.27 = bf16[128,2048]{1,0:T(8,128)(2,1)} collective-permute-done((bf16[128,2048]{1,0:T(8,128)(2,1)}, bf16[128,2048]{1,0:T(8,128)(2,1)}, u32[]{:S(2)}, u32[]{:S(2)}) %collective-permute-start.27) | collective-permute-done | bytes 524320 | tf_op jit(solution)/shard_map/ppermute | solution.py:28
  310.5 9.0 %collective-permute-done.26 = bf16[128,2048]{1,0:T(8,128)(2,1)} collective-permute-done((bf16[128,2048]{1,0:T(8,128)(2,1)}, bf16[128,2048]{1,0:T(8,128)(2,1)}, u32[]{:S(2)}, u32[]{:S(2)}) %collective-permute-start.26) | collective-permute-done | bytes 524320 | tf_op jit(solution)/shard_map/ppermute | solution.py:28
  321.2 4.3 fusion.71
  327.2 3.5 fusion.63
  330.7 3.5 convolution_add_fusion
  334.2 3.6 fusion.73
  337.9 4.7 multiply_convert_fusion.2
  346.3 3.6 fusion.204
  350.0 3.6 add_convert_fusion.2
  354.5 3.2 collective-permute-start.53
  357.9 3.6 convolution_convert_fusion.4
  361.6 3.6 convolution_convert_fusion.3
  366.4 3.1 collective-permute-start.45
  369.5 3.2 convolution_convert_fusion.1
  372.7 14.2 %collective-permute-done.54 = bf16[128,2048]{1,0:T(8,128)(2,1)S(1)} collective-permute-done((bf16[128,2048]{1,0:T(8,128)(2,1)S(1)}, bf16[128,2048]{1,0:T(8,128)(2,1)S(1)}, u32[]{:S(2)}, u32[]{:S(2)}) %collective-permute-start.54) | collective-permute-done | bytes 524320 | tf_op jit(solution)/shard_map/ppermute | solution.py:28
  389.3 10.9 %collective-permute-done.46 = bf16[128,2048]{1,0:T(8,128)(2,1)S(1)} collective-permute-done((bf16[128,2048]{1,0:T(8,128)(2,1)S(1)}, bf16[128,2048]{1,0:T(8,128)(2,1)S(1)}, u32[]{:S(2)}, u32[]{:S(2)}) %collective-permute-start.46) | collective-permute-done | bytes 524320 | tf_op jit(solution)/shard_map/ppermute | solution.py:28
  404.0 3.2 collective-permute-start.56
  415.5 12.0 %collective-permute-done.57 = bf16[128,2048]{1,0:T(8,128)(2,1)S(1)} collective-permute-done((bf16[128,2048]{1,0:T(8,128)(2,1)S(1)}, bf16[128,2048]{1,0:T(8,128)(2,1)S(1)}, u32[]{:S(2)}, u32[]{:S(2)}) %collective-permute-start.57) | collective-permute-done | bytes 524320 | tf_op jit(solution)/shard_map/ppermute | solution.py:28
  445.1 4.3 collective-permute-start.59
  465.3 2.4 collective-permute-start.61
  475.6 15.8 %collective-permute-done.62 = bf16[128,2048]{1,0:T(8,128)(2,1)S(1)} collective-permute-done((bf16[128,2048]{1,0:T(8,128)(2,1)S(1)}, bf16[128,2048]{1,0:T(8,128)(2,1)S(1)}, u32[]{:S(2)}, u32[]{:S(2)}) %collective-permute-start.62) | collective-permute-done | bytes 524320 | tf_op jit(solution)/shard_map/ppermute | solution.py:28
  507.5 2.7 collective-permute-start.67
  512.8 2.6 collective-permute-start.71
  526.3 5.5 collective-permute-start.63
  537.0 3.4 convert_add_fusion
  549.2 3.9 pad_maximum_fusion.1
  559.6 3.4 collective-permute-start.76
  568.6 3.9 collective-permute-done.78
  574.9 9.9 %collective-permute-done.76 = bf16[512,512]{1,0:T(8,128)(2,1)S(1)} collective-permute-done((bf16[512,512]{1,0:T(8,128)(2,1)S(1)}, bf16[512,512]{1,0:T(8,128)(2,1)S(1)}, u32[]{:S(2)}, u32[]{:S(2)}) %collective-permute-start.76) | collective-permute-done | bytes 524320 | tf_op jit(solution)/shard_map/ppermute | solution.py:28
  585.6 28.6 %collective-permute-done.86 = bf16[1024,256]{1,0:T(8,128)(2,1)S(1)} collective-permute-done((bf16[1024,256]{1,0:T(8,128)(2,1)S(1)}, bf16[1024,256]{1,0:T(8,128)(2,1)S(1)}, u32[]{:S(2)}, u32[]{:S(2)}) %collective-permute-start.86) | collective-permute-done | bytes 524320 | tf_op jit(solution)/shard_map/ppermute | solution.py:28
  622.0 21.9 %collective-permute-done.80 = bf16[512,128]{1,0:T(8,128)(2,1)S(1)} collective-permute-done((bf16[512,128]{1,0:T(8,128)(2,1)S(1)}, bf16[512,128]{1,0:T(8,128)(2,1)S(1)}, u32[]{:S(2)}, u32[]{:S(2)}) %collective-permute-start.80) | collective-permute-done | bytes 131104 | tf_op jit(solution)/shard_map/ppermute | solution.py:28
  646.0 4.0 collective-permute-done.89
  654.3 2.6 collective-permute-done.87
  658.0 3.7 collective-permute-start.92
  663.2 3.0 fusion.169
  667.5 29.4 %collective-permute-done.94 = bf16[1040,512]{1,0:T(8,128)(2,1)} collective-permute-done((bf16[1040,512]{1,0:T(8,128)(2,1)}, bf16[1040,512]{1,0:T(8,128)(2,1)}, u32[]{:S(2)}, u32[]{:S(2)}) %collective-permute-start.94) | collective-permute-done | bytes 1064992 | tf_op jit(solution)/shard_map/ppermute | solution.py:28
  696.8 4.5 collective-permute-start.102
  701.3 6.8 collective-permute-done.92
  716.3 4.7 collective-permute-done.97
  (702 shorter events, 278.5 us)
Async XLA Ops:
  3.1 43.6 %collective-permute-start.15 = (bf16[512,128]{1,0:T(8,128)(2,1)}, bf16[512,128]{1,0:T(8,128)(2,1)}, u32[]{:S(2)}, u32[]{:S(2)}) collective-permute-start(bf16[512,128]{1,0:T(8,128)(2,1)} %pad_maximum_fusion.40), channel_id=1, source_target_pairs={{0,20},{4,16},{16,4},{20,0},{1,21},{5,17},{17,5},{21,1},{2,22},{6,... | collective-permute-start | bytes 393224 | tf_op jit(solution)/shard_map/ppermute | solution.py:28
  6.2 41.0 %collective-permute-start.14 = (bf16[512,128]{1,0:T(8,128)(2,1)}, bf16[512,128]{1,0:T(8,128)(2,1)}, u32[]{:S(2)}, u32[]{:S(2)}) collective-permute-start(bf16[512,128]{1,0:T(8,128)(2,1)} %pad_maximum_fusion.40), channel_id=1, source_target_pairs={{0,4},{4,0},{16,20},{20,16},{1,5},{5,1},{17,21},{21,17},{2,6},{6,2... | collective-permute-start | bytes 393224 | tf_op jit(solution)/shard_map/ppermute | solution.py:28
  6.9 43.5 %collective-permute-start.13 = (bf16[512,128]{1,0:T(8,128)(2,1)}, bf16[512,128]{1,0:T(8,128)(2,1)}, u32[]{:S(2)}, u32[]{:S(2)}) collective-permute-start(bf16[512,128]{1,0:T(8,128)(2,1)} %pad_maximum_fusion.40), channel_id=1, source_target_pairs={{0,16},{4,20},{16,0},{20,4},{1,17},{5,21},{17,1},{21,5},{2,18},{6,... | collective-permute-start | bytes 393224 | tf_op jit(solution)/shard_map/ppermute | solution.py:28
  8.8 42.2 %collective-permute-start.6 = (bf16[512,128]{0,1:T(8,128)(2,1)}, bf16[512,128]{0,1:T(8,128)(2,1)}, u32[]{:S(2)}, u32[]{:S(2)}) collective-permute-start(bf16[512,128]{0,1:T(8,128)(2,1)} %get-tuple-element.175), channel_id=1, source_target_pairs={{0,96},{32,64},{64,32},{96,0},{1,97},{33,65},{65,33},{97,1},{2,98}... | collective-permute-start | bytes 393224 | tf_op jit(solution)/shard_map/ppermute | solution.py:28
  12.3 31.3 %collective-permute-start.11 = (s32[2,1024]{1,0:T(2,128)S(1)}, s32[2,1024]{1,0:T(2,128)S(1)}, u32[]{:S(2)}, u32[]{:S(2)}) collective-permute-start(s32[2,1024]{1,0:T(2,128)S(1)} %pad_add_fusion), channel_id=1, source_target_pairs={{0,8},{8,0},{1,9},{9,1},{2,10},{10,2},{3,11},{11,3},{4,12},{12,4},... | collective-permute-start | bytes 24584 | tf_op jit(solution)/shard_map/ppermute | solution.py:28
  64.9 67.1 %collective-permute-start = (f32[128,2048]{1,0:T(8,128)S(1)}, f32[128,2048]{1,0:T(8,128)S(1)}, u32[]{:S(2)}, u32[]{:S(2)}) collective-permute-start(f32[128,2048]{1,0:T(8,128)S(1)} %copy-done.95), channel_id=1, source_target_pairs={{0,0},{4,8},{8,4},{12,12},{1,1},{5,9},{9,5},{13,13},{2,2},{6,10},{... | collective-permute-start | bytes 3145736 | tf_op jit(solution)/shard_map/ppermute | solution.py:48
  68.2 43.4 %collective-permute-start.18 = (bf16[1024,256]{1,0:T(8,128)(2,1)S(1)}, bf16[1024,256]{1,0:T(8,128)(2,1)S(1)}, u32[]{:S(2)}, u32[]{:S(2)}) collective-permute-start(bf16[1024,256]{1,0:T(8,128)(2,1)S(1)} %maximum_maximum_fusion.1), channel_id=1, source_target_pairs={{0,96},{32,64},{64,32},{96,0},{1,97},{33,65},{65,33},{97,1},{2,98}... | collective-permute-start | bytes 1572872 | tf_op jit(solution)/shard_map/ppermute | solution.py:28
  71.0 42.8 %collective-permute-start.17 = (bf16[1024,256]{1,0:T(8,128)(2,1)S(1)}, bf16[1024,256]{1,0:T(8,128)(2,1)S(1)}, u32[]{:S(2)}, u32[]{:S(2)}) collective-permute-start(bf16[1024,256]{1,0:T(8,128)(2,1)S(1)} %maximum_maximum_fusion.1), channel_id=1, source_target_pairs={{0,64},{32,96},{64,0},{96,32},{1,65},{33,97},{65,1},{97,33},{2,66}... | collective-permute-start | bytes 1572872 | tf_op jit(solution)/shard_map/ppermute | solution.py:28
  71.0 35.8 %collective-permute-start.8 = (bf16[512,512]{0,1:T(8,128)(2,1)S(1)}, bf16[512,512]{0,1:T(8,128)(2,1)S(1)}, u32[]{:S(2)}, u32[]{:S(2)}) collective-permute-start(bf16[512,512]{0,1:T(8,128)(2,1)S(1)} %pad_maximum_fusion.28), channel_id=1, source_target_pairs={{0,4},{4,0},{16,20},{20,16},{1,5},{5,1},{17,21},{21,17},{2,6},{6,2... | collective-permute-start | bytes 1572872 | tf_op jit(solution)/shard_map/ppermute | solution.py:28
  77.2 32.7 %collective-permute-start.9 = (bf16[512,512]{0,1:T(8,128)(2,1)S(1)}, bf16[512,512]{0,1:T(8,128)(2,1)S(1)}, u32[]{:S(2)}, u32[]{:S(2)}) collective-permute-start(bf16[512,512]{0,1:T(8,128)(2,1)S(1)} %pad_maximum_fusion.28), channel_id=1, source_target_pairs={{0,20},{4,16},{16,4},{20,0},{1,21},{5,17},{17,5},{21,1},{2,22},{6,... | collective-permute-start | bytes 1572872 | tf_op jit(solution)/shard_map/ppermute | solution.py:28
  111.6 48.7 %collective-permute-start.41 = (bf16[2048,256]{1,0:T(8,128)(2,1)S(1)}, bf16[2048,256]{1,0:T(8,128)(2,1)S(1)}, u32[]{:S(2)}, u32[]{:S(2)}) collective-permute-start(bf16[2048,256]{1,0:T(8,128)(2,1)S(1)} %maximum_maximum_fusion), channel_id=1, source_target_pairs={{0,96},{32,64},{64,32},{96,0},{1,97},{33,65},{65,33},{97,1},{2,98}... | collective-permute-start | bytes 3145736 | tf_op jit(solution)/shard_map/ppermute | solution.py:28
  113.8 46.8 %collective-permute-start.40 = (bf16[2048,256]{1,0:T(8,128)(2,1)S(1)}, bf16[2048,256]{1,0:T(8,128)(2,1)S(1)}, u32[]{:S(2)}, u32[]{:S(2)}) collective-permute-start(bf16[2048,256]{1,0:T(8,128)(2,1)S(1)} %maximum_maximum_fusion), channel_id=1, source_target_pairs={{0,64},{32,96},{64,0},{96,32},{1,65},{33,97},{65,1},{97,33},{2,66}... | collective-permute-start | bytes 3145736 | tf_op jit(solution)/shard_map/ppermute | solution.py:28
  116.9 44.5 %collective-permute-start.39 = (bf16[2048,256]{1,0:T(8,128)(2,1)S(1)}, bf16[2048,256]{1,0:T(8,128)(2,1)S(1)}, u32[]{:S(2)}, u32[]{:S(2)}) collective-permute-start(bf16[2048,256]{1,0:T(8,128)(2,1)S(1)} %maximum_maximum_fusion), channel_id=1, source_target_pairs={{0,32},{32,0},{64,96},{96,64},{1,33},{33,1},{65,97},{97,65},{2,34}... | collective-permute-start | bytes 3145736 | tf_op jit(solution)/shard_map/ppermute | solution.py:28
  123.7 48.1 %collective-permute-start.33 = (bf16[1040,512]{1,0:T(8,128)(2,1)S(1)}, bf16[1040,512]{1,0:T(8,128)(2,1)S(1)}, u32[]{:S(2)}, u32[]{:S(2)}) collective-permute-start(bf16[1040,512]{1,0:T(8,128)(2,1)S(1)} %pad_maximum_fusion.14), channel_id=1, source_target_pairs={{0,4},{4,0},{16,20},{20,16},{1,5},{5,1},{17,21},{21,17},{2,6},{6,2... | collective-permute-start | bytes 3194888 | tf_op jit(solution)/shard_map/ppermute | solution.py:28
  132.1 43.9 %collective-permute-start.34 = (bf16[1040,512]{1,0:T(8,128)(2,1)S(1)}, bf16[1040,512]{1,0:T(8,128)(2,1)S(1)}, u32[]{:S(2)}, u32[]{:S(2)}) collective-permute-start(bf16[1040,512]{1,0:T(8,128)(2,1)S(1)} %pad_maximum_fusion.14), channel_id=1, source_target_pairs={{0,20},{4,16},{16,4},{20,0},{1,21},{5,17},{17,5},{21,1},{2,22},{6,... | collective-permute-start | bytes 3194888 | tf_op jit(solution)/shard_map/ppermute | solution.py:28
  160.3 24.4 %collective-permute-start.32 = (bf16[1040,512]{1,0:T(8,128)(2,1)S(1)}, bf16[1040,512]{1,0:T(8,128)(2,1)S(1)}, u32[]{:S(2)}, u32[]{:S(2)}) collective-permute-start(bf16[1040,512]{1,0:T(8,128)(2,1)S(1)} %pad_maximum_fusion.14), channel_id=1, source_target_pairs={{0,16},{4,20},{16,0},{20,4},{1,17},{5,21},{17,1},{21,5},{2,18},{6,... | collective-permute-start | bytes 3194888 | tf_op jit(solution)/shard_map/ppermute | solution.py:28
  160.6 42.4 %collective-permute-start.19 = (bf16[512,1024]{1,0:T(8,128)(2,1)S(1)}, bf16[512,1024]{1,0:T(8,128)(2,1)S(1)}, u32[]{:S(2)}, u32[]{:S(2)}) collective-permute-start(bf16[512,1024]{1,0:T(8,128)(2,1)S(1)} %pad_maximum_fusion.20), channel_id=1, source_target_pairs={{0,8},{8,0},{1,9},{9,1},{2,10},{10,2},{3,11},{11,3},{4,12},{12,4},... | collective-permute-start | bytes 3145736 | tf_op jit(solution)/shard_map/ppermute | solution.py:28
  161.4 46.4 %collective-permute-start.10 = (bf16[512,1024]{0,1:T(8,128)(2,1)}, bf16[512,1024]{0,1:T(8,128)(2,1)}, u32[]{:S(2)}, u32[]{:S(2)}) collective-permute-start(bf16[512,1024]{0,1:T(8,128)(2,1)} %pad_maximum_fusion.18), channel_id=1, source_target_pairs={{0,8},{8,0},{1,9},{9,1},{2,10},{10,2},{3,11},{11,3},{4,12},{12,4},... | collective-permute-start | bytes 3145736 | tf_op jit(solution)/shard_map/ppermute | solution.py:28
  171.8 27.4 %collective-permute-start.3 = (bf16[128,2048]{1,0:T(8,128)(2,1)S(1)}, bf16[128,2048]{1,0:T(8,128)(2,1)S(1)}, u32[]{:S(2)}, u32[]{:S(2)}) collective-permute-start(bf16[128,2048]{1,0:T(8,128)(2,1)S(1)} %multiply_convert_fusion.5), channel_id=1, source_target_pairs={{0,3},{1,2},{2,1},{3,0},{4,7},{5,6},{6,5},{7,4},{8,11},{9,10},{10,... | collective-permute-start | bytes 1572872 | tf_op jit(solution)/shard_map/ppermute | solution.py:28
  176.0 26.2 %collective-permute-start.2 = (bf16[128,2048]{1,0:T(8,128)(2,1)S(1)}, bf16[128,2048]{1,0:T(8,128)(2,1)S(1)}, u32[]{:S(2)}, u32[]{:S(2)}) collective-permute-start(bf16[128,2048]{1,0:T(8,128)(2,1)S(1)} %multiply_convert_fusion.5), channel_id=1, source_target_pairs={{0,2},{1,3},{2,0},{3,1},{4,6},{5,7},{6,4},{7,5},{8,10},{9,11},{10,... | collective-permute-start | bytes 1572872 | tf_op jit(solution)/shard_map/ppermute | solution.py:28
  199.2 73.4 %collective-permute-start.51 = (bf16[128,2048]{1,0:T(8,128)(2,1)}, bf16[128,2048]{1,0:T(8,128)(2,1)}, u32[]{:S(2)}, u32[]{:S(2)}) collective-permute-start(bf16[128,2048]{1,0:T(8,128)(2,1)} %constant_dynamic-update-slice_fusion.63), channel_id=1, source_target_pairs={{0,3},{1,2},{2,1},{3,0},{4,7},{5,6},{6,5},{7,4},{8,11},{9,10},{10,... | collective-permute-start | bytes 1572872 | tf_op jit(solution)/shard_map/ppermute | solution.py:28
  202.2 38.2 %collective-permute-start.22 = (bf16[512,1024]{1,0:T(8,128)(2,1)}, bf16[512,1024]{1,0:T(8,128)(2,1)}, u32[]{:S(2)}, u32[]{:S(2)}) collective-permute-start(bf16[512,1024]{1,0:T(8,128)(2,1)} %pad_maximum_fusion.21), channel_id=1, source_target_pairs={{0,8},{8,0},{1,9},{9,1},{2,10},{10,2},{3,11},{11,3},{4,12},{12,4},... | collective-permute-start | bytes 3145736 | tf_op jit(solution)/shard_map/ppermute | solution.py:28
  203.0 118.1 %collective-permute-start.42 = (bf16[1376,1024]{1,0:T(8,128)(2,1)}, bf16[1376,1024]{1,0:T(8,128)(2,1)}, u32[]{:S(2)}, u32[]{:S(2)}) collective-permute-start(bf16[1376,1024]{1,0:T(8,128)(2,1)} %pad_maximum_fusion.6), channel_id=1, source_target_pairs={{0,8},{8,0},{1,9},{9,1},{2,10},{10,2},{3,11},{11,3},{4,12},{12,4},... | collective-permute-start | bytes 8454152 | tf_op jit(solution)/shard_map/ppermute | solution.py:28
  242.7 26.9 %collective-permute-start.25 = (bf16[128,2048]{1,0:T(8,128)(2,1)S(1)}, bf16[128,2048]{1,0:T(8,128)(2,1)S(1)}, u32[]{:S(2)}, u32[]{:S(2)}) collective-permute-start(bf16[128,2048]{1,0:T(8,128)(2,1)S(1)} %get-tuple-element.110), channel_id=1, source_target_pairs={{0,3},{1,2},{2,1},{3,0},{4,7},{5,6},{6,5},{7,4},{8,11},{9,10},{10,... | collective-permute-start | bytes 1572872 | tf_op jit(solution)/shard_map/ppermute | solution.py:28
  243.4 26.9 %collective-permute-start.24 = (bf16[128,2048]{1,0:T(8,128)(2,1)S(1)}, bf16[128,2048]{1,0:T(8,128)(2,1)S(1)}, u32[]{:S(2)}, u32[]{:S(2)}) collective-permute-start(bf16[128,2048]{1,0:T(8,128)(2,1)S(1)} %get-tuple-element.111), channel_id=1, source_target_pairs={{0,2},{1,3},{2,0},{3,1},{4,6},{5,7},{6,4},{7,5},{8,10},{9,11},{10,... | collective-permute-start | bytes 1572872 | tf_op jit(solution)/shard_map/ppermute | solution.py:28
  244.8 26.3 %collective-permute-start.23 = (bf16[128,2048]{1,0:T(8,128)(2,1)S(1)}, bf16[128,2048]{1,0:T(8,128)(2,1)S(1)}, u32[]{:S(2)}, u32[]{:S(2)}) collective-permute-start(bf16[128,2048]{1,0:T(8,128)(2,1)S(1)} %get-tuple-element.109), channel_id=1, source_target_pairs={{0,1},{1,0},{2,3},{3,2},{4,5},{5,4},{6,7},{7,6},{8,9},{9,8},{10,11... | collective-permute-start | bytes 1572872 | tf_op jit(solution)/shard_map/ppermute | solution.py:28
  270.3 23.5 %collective-permute-start.49 = (bf16[128,2048]{1,0:T(8,128)(2,1)}, bf16[128,2048]{1,0:T(8,128)(2,1)}, u32[]{:S(2)}, u32[]{:S(2)}) collective-permute-start(bf16[128,2048]{1,0:T(8,128)(2,1)} %constant_dynamic-update-slice_fusion.63), channel_id=1, source_target_pairs={{0,1},{1,0},{2,3},{3,2},{4,5},{5,4},{6,7},{7,6},{8,9},{9,8},{10,11... | collective-permute-start | bytes 1572872 | tf_op jit(solution)/shard_map/ppermute | solution.py:28
  271.1 56.1 %collective-permute-start.43 = (bf16[1376,1024]{1,0:T(8,128)(2,1)}, bf16[1376,1024]{1,0:T(8,128)(2,1)}, u32[]{:S(2)}, u32[]{:S(2)}) collective-permute-start(bf16[1376,1024]{1,0:T(8,128)(2,1)} %fusion.21), channel_id=1, source_target_pairs={{0,8},{8,0},{1,9},{9,1},{2,10},{10,2},{3,11},{11,3},{4,12},{12,4},... | collective-permute-start | bytes 8454152 | tf_op jit(solution)/shard_map/ppermute | solution.py:28
  272.6 24.4 %collective-permute-start.28 = (bf16[128,2048]{1,0:T(8,128)(2,1)}, bf16[128,2048]{1,0:T(8,128)(2,1)}, u32[]{:S(2)}, u32[]{:S(2)}) collective-permute-start(bf16[128,2048]{1,0:T(8,128)(2,1)} %multiply_convert_fusion.4), channel_id=1, source_target_pairs={{0,3},{1,2},{2,1},{3,0},{4,7},{5,6},{6,5},{7,4},{8,11},{9,10},{10,... | collective-permute-start | bytes 1572872 | tf_op jit(solution)/shard_map/ppermute | solution.py:28
  287.1 47.1 %collective-permute-start.35 = (bf16[1376,1024]{1,0:T(8,128)(2,1)}, bf16[1376,1024]{1,0:T(8,128)(2,1)}, u32[]{:S(2)}, u32[]{:S(2)}) collective-permute-start(bf16[1376,1024]{1,0:T(8,128)(2,1)} %pad_maximum_fusion.5), channel_id=1, source_target_pairs={{0,8},{8,0},{1,9},{9,1},{2,10},{10,2},{3,11},{11,3},{4,12},{12,4},... | collective-permute-start | bytes 8454152 | tf_op jit(solution)/shard_map/ppermute | solution.py:28
  297.0 22.4 %collective-permute-start.26 = (bf16[128,2048]{1,0:T(8,128)(2,1)}, bf16[128,2048]{1,0:T(8,128)(2,1)}, u32[]{:S(2)}, u32[]{:S(2)}) collective-permute-start(bf16[128,2048]{1,0:T(8,128)(2,1)} %multiply_convert_fusion.4), channel_id=1, source_target_pairs={{0,1},{1,0},{2,3},{3,2},{4,5},{5,4},{6,7},{7,6},{8,9},{9,8},{10,11... | collective-permute-start | bytes 1572872 | tf_op jit(solution)/shard_map/ppermute | solution.py:28
  353.7 33.2 %collective-permute-start.54 = (bf16[128,2048]{1,0:T(8,128)(2,1)S(1)}, bf16[128,2048]{1,0:T(8,128)(2,1)S(1)}, u32[]{:S(2)}, u32[]{:S(2)}) collective-permute-start(bf16[128,2048]{1,0:T(8,128)(2,1)S(1)} %get-tuple-element.104), channel_id=1, source_target_pairs={{0,3},{1,2},{2,1},{3,0},{4,7},{5,6},{6,5},{7,4},{8,11},{9,10},{10,... | collective-permute-start | bytes 1572872 | tf_op jit(solution)/shard_map/ppermute | solution.py:28
  354.5 34.1 %collective-permute-start.53 = (bf16[128,2048]{1,0:T(8,128)(2,1)S(1)}, bf16[128,2048]{1,0:T(8,128)(2,1)S(1)}, u32[]{:S(2)}, u32[]{:S(2)}) collective-permute-start(bf16[128,2048]{1,0:T(8,128)(2,1)S(1)} %get-tuple-element.105), channel_id=1, source_target_pairs={{0,2},{1,3},{2,0},{3,1},{4,6},{5,7},{6,4},{7,5},{8,10},{9,11},{10,... | collective-permute-start | bytes 1572872 | tf_op jit(solution)/shard_map/ppermute | solution.py:28
  357.7 30.9 %collective-permute-start.52 = (bf16[128,2048]{1,0:T(8,128)(2,1)S(1)}, bf16[128,2048]{1,0:T(8,128)(2,1)S(1)}, u32[]{:S(2)}, u32[]{:S(2)}) collective-permute-start(bf16[128,2048]{1,0:T(8,128)(2,1)S(1)} %get-tuple-element.103), channel_id=1, source_target_pairs={{0,1},{1,0},{2,3},{3,2},{4,5},{5,4},{6,7},{7,6},{8,9},{9,8},{10,11... | collective-permute-start | bytes 1572872 | tf_op jit(solution)/shard_map/ppermute | solution.py:28
  365.3 34.9 %collective-permute-start.46 = (bf16[128,2048]{1,0:T(8,128)(2,1)S(1)}, bf16[128,2048]{1,0:T(8,128)(2,1)S(1)}, u32[]{:S(2)}, u32[]{:S(2)}) collective-permute-start(bf16[128,2048]{1,0:T(8,128)(2,1)S(1)} %get-tuple-element.107), channel_id=1, source_target_pairs={{0,3},{1,2},{2,1},{3,0},{4,7},{5,6},{6,5},{7,4},{8,11},{9,10},{10,... | collective-permute-start | bytes 1572872 | tf_op jit(solution)/shard_map/ppermute | solution.py:28
  366.4 33.9 %collective-permute-start.45 = (bf16[128,2048]{1,0:T(8,128)(2,1)S(1)}, bf16[128,2048]{1,0:T(8,128)(2,1)S(1)}, u32[]{:S(2)}, u32[]{:S(2)}) collective-permute-start(bf16[128,2048]{1,0:T(8,128)(2,1)S(1)} %get-tuple-element.108), channel_id=1, source_target_pairs={{0,2},{1,3},{2,0},{3,1},{4,6},{5,7},{6,4},{7,5},{8,10},{9,11},{10,... | collective-permute-start | bytes 1572872 | tf_op jit(solution)/shard_map/ppermute | solution.py:28
  402.9 24.6 %collective-permute-start.57 = (bf16[128,2048]{1,0:T(8,128)(2,1)S(1)}, bf16[128,2048]{1,0:T(8,128)(2,1)S(1)}, u32[]{:S(2)}, u32[]{:S(2)}) collective-permute-start(bf16[128,2048]{1,0:T(8,128)(2,1)S(1)} %get-tuple-element.46), channel_id=1, source_target_pairs={{0,3},{1,2},{2,1},{3,0},{4,7},{5,6},{6,5},{7,4},{8,11},{9,10},{10,... | collective-permute-start | bytes 1572872 | tf_op jit(solution)/shard_map/ppermute | solution.py:28
  404.0 23.6 %collective-permute-start.56 = (bf16[128,2048]{1,0:T(8,128)(2,1)S(1)}, bf16[128,2048]{1,0:T(8,128)(2,1)S(1)}, u32[]{:S(2)}, u32[]{:S(2)}) collective-permute-start(bf16[128,2048]{1,0:T(8,128)(2,1)S(1)} %get-tuple-element.46), channel_id=1, source_target_pairs={{0,2},{1,3},{2,0},{3,1},{4,6},{5,7},{6,4},{7,5},{8,10},{9,11},{10,... | collective-permute-start | bytes 1572872 | tf_op jit(solution)/shard_map/ppermute | solution.py:28
  407.2 20.9 %collective-permute-start.55 = (bf16[128,2048]{1,0:T(8,128)(2,1)S(1)}, bf16[128,2048]{1,0:T(8,128)(2,1)S(1)}, u32[]{:S(2)}, u32[]{:S(2)}) collective-permute-start(bf16[128,2048]{1,0:T(8,128)(2,1)S(1)} %get-tuple-element.46), channel_id=1, source_target_pairs={{0,1},{1,0},{2,3},{3,2},{4,5},{5,4},{6,7},{7,6},{8,9},{9,8},{10,11... | collective-permute-start | bytes 1572872 | tf_op jit(solution)/shard_map/ppermute | solution.py:28
  433.2 22.3 %collective-permute-start.47 = (f32[128,2048]{1,0:T(8,128)}, f32[128,2048]{1,0:T(8,128)S(1)}, u32[]{:S(2)}, u32[]{:S(2)}) collective-permute-start(f32[128,2048]{1,0:T(8,128)} %constant_dynamic-update-slice_fusion.47), channel_id=1, source_target_pairs={{0,0},{4,8},{8,4},{12,12},{1,1},{5,9},{9,5},{13,13},{2,2},{6,10},{... | collective-permute-start | bytes 3145736 | tf_op jit(solution)/shard_map/ppermute | solution.py:48
  451.0 73.1 %collective-permute-start.91 = (bf16[1376,1024]{1,0:T(8,128)(2,1)S(1)}, bf16[1376,1024]{1,0:T(8,128)(2,1)S(1)}, u32[]{:S(2)}, u32[]{:S(2)}) collective-permute-start(bf16[1376,1024]{1,0:T(8,128)(2,1)S(1)} %copy-done.94), channel_id=1, source_target_pairs={{0,8},{8,0},{1,9},{9,1},{2,10},{10,2},{3,11},{11,3},{4,12},{12,4},... | collective-permute-start | bytes 8454152 | tf_op jit(solution)/shard_map/ppermute | solution.py:28
  452.5 73.9 %collective-permute-start.90 = (bf16[1376,1024]{1,0:T(8,128)(2,1)S(1)}, bf16[1376,1024]{1,0:T(8,128)(2,1)S(1)}, u32[]{:S(2)}, u32[]{:S(2)}) collective-permute-start(bf16[1376,1024]{1,0:T(8,128)(2,1)S(1)} %convolution_convert_fusion.2), channel_id=1, source_target_pairs={{0,8},{8,0},{1,9},{9,1},{2,10},{10,2},{3,11},{11,3},{4,12},{12,4},... | collective-permute-start | bytes 8454152 | tf_op jit(solution)/shard_map/ppermute | solution.py:28
  464.9 26.4 %collective-permute-start.62 = (bf16[128,2048]{1,0:T(8,128)(2,1)S(1)}, bf16[128,2048]{1,0:T(8,128)(2,1)S(1)}, u32[]{:S(2)}, u32[]{:S(2)}) collective-permute-start(bf16[128,2048]{1,0:T(8,128)(2,1)S(1)} %get-tuple-element.101), channel_id=1, source_target_pairs={{0,3},{1,2},{2,1},{3,0},{4,7},{5,6},{6,5},{7,4},{8,11},{9,10},{10,... | collective-permute-start | bytes 1572872 | tf_op jit(solution)/shard_map/ppermute | solution.py:28
  465.3 26.0 %collective-permute-start.61 = (bf16[128,2048]{1,0:T(8,128)(2,1)S(1)}, bf16[128,2048]{1,0:T(8,128)(2,1)S(1)}, u32[]{:S(2)}, u32[]{:S(2)}) collective-permute-start(bf16[128,2048]{1,0:T(8,128)(2,1)S(1)} %get-tuple-element.102), channel_id=1, source_target_pairs={{0,2},{1,3},{2,0},{3,1},{4,6},{5,7},{6,4},{7,5},{8,10},{9,11},{10,... | collective-permute-start | bytes 1572872 | tf_op jit(solution)/shard_map/ppermute | solution.py:28
  471.1 20.8 %collective-permute-start.60 = (bf16[128,2048]{1,0:T(8,128)(2,1)S(1)}, bf16[128,2048]{1,0:T(8,128)(2,1)S(1)}, u32[]{:S(2)}, u32[]{:S(2)}) collective-permute-start(bf16[128,2048]{1,0:T(8,128)(2,1)S(1)} %get-tuple-element.100), channel_id=1, source_target_pairs={{0,1},{1,0},{2,3},{3,2},{4,5},{5,4},{6,7},{7,6},{8,9},{9,8},{10,11... | collective-permute-start | bytes 1572872 | tf_op jit(solution)/shard_map/ppermute | solution.py:28
  520.4 32.8 %collective-permute-start.75 = (bf16[512,1024]{1,0:T(8,128)(2,1)}, bf16[512,1024]{1,0:T(8,128)(2,1)}, u32[]{:S(2)}, u32[]{:S(2)}) collective-permute-start(bf16[512,1024]{1,0:T(8,128)(2,1)} %convolution_convert_fusion.7), channel_id=1, source_target_pairs={{0,8},{8,0},{1,9},{9,1},{2,10},{10,2},{3,11},{11,3},{4,12},{12,4},... | collective-permute-start | bytes 3145736 | tf_op jit(solution)/shard_map/ppermute | solution.py:28
  523.3 31.8 %collective-permute-start.74 = (bf16[512,1024]{1,0:T(8,128)(2,1)}, bf16[512,1024]{1,0:T(8,128)(2,1)}, u32[]{:S(2)}, u32[]{:S(2)}) collective-permute-start(bf16[512,1024]{1,0:T(8,128)(2,1)} %convolution_convert_fusion.8), channel_id=1, source_target_pairs={{0,8},{8,0},{1,9},{9,1},{2,10},{10,2},{3,11},{11,3},{4,12},{12,4},... | collective-permute-start | bytes 3145736 | tf_op jit(solution)/shard_map/ppermute | solution.py:28
  524.1 35.5 %collective-permute-start.82 = (bf16[512,1024]{1,0:T(8,128)(2,1)}, bf16[512,1024]{1,0:T(8,128)(2,1)}, u32[]{:S(2)}, u32[]{:S(2)}) collective-permute-start(bf16[512,1024]{1,0:T(8,128)(2,1)} %convolution_convert_fusion.6), channel_id=1, source_target_pairs={{0,8},{8,0},{1,9},{9,1},{2,10},{10,2},{3,11},{11,3},{4,12},{12,4},... | collective-permute-start | bytes 3145736 | tf_op jit(solution)/shard_map/ppermute | solution.py:28
  526.3 39.3 %collective-permute-start.63 = (bf16[128,2048]{1,0:T(8,128)(2,1)}, bf16[128,2048]{1,0:T(8,128)(2,1)}, u32[]{:S(2)}, u32[]{:S(2)}) collective-permute-start(bf16[128,2048]{1,0:T(8,128)(2,1)} %constant_dynamic-update-slice_fusion.79), channel_id=1, source_target_pairs={{0,0},{4,8},{8,4},{12,12},{1,1},{5,9},{9,5},{13,13},{2,2},{6,10},{... | collective-permute-start | bytes 1572872 | tf_op jit(solution)/shard_map/ppermute | solution.py:48
  543.4 114.6 %collective-permute-start.101 = (bf16[2048,256]{1,0:T(8,128)(2,1)}, bf16[2048,256]{1,0:T(8,128)(2,1)}, u32[]{:S(2)}, u32[]{:S(2)}) collective-permute-start(bf16[2048,256]{1,0:T(8,128)(2,1)} %get-tuple-element.71), channel_id=1, source_target_pairs={{0,96},{32,64},{64,32},{96,0},{1,97},{33,65},{65,33},{97,1},{2,98}... | collective-permute-start | bytes 3145736 | tf_op jit(solution)/shard_map/ppermute | solution.py:28
  559.6 25.2 %collective-permute-start.76 = (bf16[512,512]{1,0:T(8,128)(2,1)S(1)}, bf16[512,512]{1,0:T(8,128)(2,1)S(1)}, u32[]{:S(2)}, u32[]{:S(2)}) collective-permute-start(bf16[512,512]{1,0:T(8,128)(2,1)S(1)} %pad_maximum_fusion.33), channel_id=1, source_target_pairs={{0,4},{4,0},{16,20},{20,16},{1,5},{5,1},{17,21},{21,17},{2,6},{6,2... | collective-permute-start | bytes 1572872 | tf_op jit(solution)/shard_map/ppermute | solution.py:28
  565.7 97.5 %collective-permute-start.100 = (bf16[2048,256]{1,0:T(8,128)(2,1)}, bf16[2048,256]{1,0:T(8,128)(2,1)}, u32[]{:S(2)}, u32[]{:S(2)}) collective-permute-start(bf16[2048,256]{1,0:T(8,128)(2,1)} %get-tuple-element.72), channel_id=1, source_target_pairs={{0,64},{32,96},{64,0},{96,32},{1,65},{33,97},{65,1},{97,33},{2,66}... | collective-permute-start | bytes 3145736 | tf_op jit(solution)/shard_map/ppermute | solution.py:28
  572.6 41.6 %collective-permute-start.86 = (bf16[1024,256]{1,0:T(8,128)(2,1)S(1)}, bf16[1024,256]{1,0:T(8,128)(2,1)S(1)}, u32[]{:S(2)}, u32[]{:S(2)}) collective-permute-start(bf16[1024,256]{1,0:T(8,128)(2,1)S(1)} %get-tuple-element.90), channel_id=1, source_target_pairs={{0,96},{32,64},{64,32},{96,0},{1,97},{33,65},{65,33},{97,1},{2,98}... | collective-permute-start | bytes 1572872 | tf_op jit(solution)/shard_map/ppermute | solution.py:28
  573.5 40.7 %collective-permute-start.85 = (bf16[1024,256]{1,0:T(8,128)(2,1)S(1)}, bf16[1024,256]{1,0:T(8,128)(2,1)S(1)}, u32[]{:S(2)}, u32[]{:S(2)}) collective-permute-start(bf16[1024,256]{1,0:T(8,128)(2,1)S(1)} %get-tuple-element.91), channel_id=1, source_target_pairs={{0,64},{32,96},{64,0},{96,32},{1,65},{33,97},{65,1},{97,33},{2,66}... | collective-permute-start | bytes 1572872 | tf_op jit(solution)/shard_map/ppermute | solution.py:28
  584.8 31.7 %collective-permute-start.84 = (bf16[1024,256]{1,0:T(8,128)(2,1)S(1)}, bf16[1024,256]{1,0:T(8,128)(2,1)S(1)}, u32[]{:S(2)}, u32[]{:S(2)}) collective-permute-start(bf16[1024,256]{1,0:T(8,128)(2,1)S(1)} %get-tuple-element.89), channel_id=1, source_target_pairs={{0,32},{32,0},{64,96},{96,64},{1,33},{33,1},{65,97},{97,65},{2,34}... | collective-permute-start | bytes 1572872 | tf_op jit(solution)/shard_map/ppermute | solution.py:28
  614.2 49.0 %collective-permute-start.99 = (bf16[2048,256]{1,0:T(8,128)(2,1)}, bf16[2048,256]{1,0:T(8,128)(2,1)}, u32[]{:S(2)}, u32[]{:S(2)}) collective-permute-start(bf16[2048,256]{1,0:T(8,128)(2,1)} %get-tuple-element.70), channel_id=1, source_target_pairs={{0,32},{32,0},{64,96},{96,64},{1,33},{33,1},{65,97},{97,65},{2,34}... | collective-permute-start | bytes 3145736 | tf_op jit(solution)/shard_map/ppermute | solution.py:28
  616.5 27.4 %collective-permute-start.80 = (bf16[512,128]{1,0:T(8,128)(2,1)S(1)}, bf16[512,128]{1,0:T(8,128)(2,1)S(1)}, u32[]{:S(2)}, u32[]{:S(2)}) collective-permute-start(bf16[512,128]{1,0:T(8,128)(2,1)S(1)} %get-tuple-element.157), channel_id=1, source_target_pairs={{0,64},{32,96},{64,0},{96,32},{1,65},{33,97},{65,1},{97,33},{2,66}... | collective-permute-start | bytes 393224 | tf_op jit(solution)/shard_map/ppermute | solution.py:28
  620.4 25.6 %collective-permute-start.79 = (bf16[512,128]{1,0:T(8,128)(2,1)S(1)}, bf16[512,128]{1,0:T(8,128)(2,1)S(1)}, u32[]{:S(2)}, u32[]{:S(2)}) collective-permute-start(bf16[512,128]{1,0:T(8,128)(2,1)S(1)} %get-tuple-element.155), channel_id=1, source_target_pairs={{0,32},{32,0},{64,96},{96,64},{1,33},{33,1},{65,97},{97,65},{2,34}... | collective-permute-start | bytes 393224 | tf_op jit(solution)/shard_map/ppermute | solution.py:28
  652.2 44.6 %collective-permute-start.94 = (bf16[1040,512]{1,0:T(8,128)(2,1)}, bf16[1040,512]{1,0:T(8,128)(2,1)}, u32[]{:S(2)}, u32[]{:S(2)}) collective-permute-start(bf16[1040,512]{1,0:T(8,128)(2,1)} %pad_maximum_fusion.17), channel_id=1, source_target_pairs={{0,20},{4,16},{16,4},{20,0},{1,21},{5,17},{17,5},{21,1},{2,22},{6,... | collective-permute-start | bytes 3194888 | tf_op jit(solution)/shard_map/ppermute | solution.py:28
  656.9 44.4 %collective-permute-start.93 = (bf16[1040,512]{1,0:T(8,128)(2,1)}, bf16[1040,512]{1,0:T(8,128)(2,1)}, u32[]{:S(2)}, u32[]{:S(2)}) collective-permute-start(bf16[1040,512]{1,0:T(8,128)(2,1)} %pad_maximum_fusion.16), channel_id=1, source_target_pairs={{0,16},{4,20},{16,0},{20,4},{1,17},{5,21},{17,1},{21,5},{2,18},{6,... | collective-permute-start | bytes 3194888 | tf_op jit(solution)/shard_map/ppermute | solution.py:28
  658.0 50.1 %collective-permute-start.92 = (bf16[1040,512]{1,0:T(8,128)(2,1)}, bf16[1040,512]{1,0:T(8,128)(2,1)S(1)}, u32[]{:S(2)}, u32[]{:S(2)}) collective-permute-start(bf16[1040,512]{1,0:T(8,128)(2,1)} %pad_maximum_fusion.15), channel_id=1, source_target_pairs={{0,4},{4,0},{16,20},{20,16},{1,5},{5,1},{17,21},{21,17},{2,6},{6,2... | collective-permute-start | bytes 3194888 | tf_op jit(solution)/shard_map/ppermute | solution.py:28
  666.3 46.0 %collective-permute-start.104 = (bf16[1024,128]{1,0:T(8,128)(2,1)S(1)}, bf16[1024,128]{1,0:T(8,128)(2,1)S(1)}, u32[]{:S(2)}, u32[]{:S(2)}) collective-permute-start(bf16[1024,128]{1,0:T(8,128)(2,1)S(1)} %get-tuple-element.133), channel_id=1, source_target_pairs={{0,20},{4,16},{16,4},{20,0},{1,21},{5,17},{17,5},{21,1},{2,22},{6,... | collective-permute-start | bytes 786440 | tf_op jit(solution)/shard_map/ppermute | solution.py:28
  667.5 47.1 %collective-permute-start.103 = (bf16[1024,128]{1,0:T(8,128)(2,1)S(1)}, bf16[1024,128]{1,0:T(8,128)(2,1)S(1)}, u32[]{:S(2)}, u32[]{:S(2)}) collective-permute-start(bf16[1024,128]{1,0:T(8,128)(2,1)S(1)} %get-tuple-element.134), channel_id=1, source_target_pairs={{0,16},{4,20},{16,0},{20,4},{1,17},{5,21},{17,1},{21,5},{2,18},{6,... | collective-permute-start | bytes 786440 | tf_op jit(solution)/shard_map/ppermute | solution.py:28
  696.8 18.6 %collective-permute-start.102 = (bf16[1024,128]{1,0:T(8,128)(2,1)S(1)}, bf16[1024,128]{1,0:T(8,128)(2,1)S(1)}, u32[]{:S(2)}, u32[]{:S(2)}) collective-permute-start(bf16[1024,128]{1,0:T(8,128)(2,1)S(1)} %get-tuple-element.132), channel_id=1, source_target_pairs={{0,4},{4,0},{16,20},{20,16},{1,5},{5,1},{17,21},{21,17},{2,6},{6,2... | collective-permute-start | bytes 786440 | tf_op jit(solution)/shard_map/ppermute | solution.py:28
  (144 other events, 2001.9 us)
